TPU v7x, 512 devices: a whole 4x8x8 slice. The times are simulated.
512 devices in a mesh: row: 32 (over z_hi, x, core), col: 16 (over y, z_lo).
Axes of the slice: x: 4, y: 8, z: 8 (z_hi: 4, z_lo: 2; z = z_hi * 2 + z_lo), core: 2. Of those that a mesh axis runs over, the one named last changes fastest.
Arguments:
- feats: bfloat16 [65536, 256], P(('row', 'col')), may hold values from -6 to 6
- tiles: bfloat16 [32, 16, 96, 128, 128], P('row', 'col')
- tile_rows: int32 [32, 16, 96], P('row', 'col'), may hold values from 0 to 15, as said below
- tile_cols: int32 [32, 16, 96], P('row', 'col'), may hold values from 0 to 31
- tile_count: int32 [32, 16], P('row', 'col'), may hold values from 12 to 96
- w_self: bfloat16 [256, 256], replicated, may hold values from -0.375 to 0.375
- w_in: bfloat16 [256, 256], replicated, may hold values from -0.375 to 0.375
- w_out: bfloat16 [256, 256], replicated, may hold values from -0.375 to 0.375
- bias: float32 [256], replicated, may hold values from -3 to 3
Outputs:
- updated: bfloat16 [65536, 256], P(('row', 'col'))
Inputs may be any that keep to these rules, and one draw needn't show every extreme that they name: `tile_rows`: within one device the live slots name distinct tile positions.
All inputs are finite; a program needn't handle non-finite values.
Results may differ from a plain program's by a relative error of at most 0.018.
Values may be sent and summed in bfloat16 or wider, within the bound.
No kernel may reach another device: no remote copies, remote signals or barrier semaphores. Data moves between devices by JAX's collectives and lax.ppermute only.
A program may use at most 64 MiB of HBM per device.

v0:
```python
import jax
import jax.numpy as jnp
from jax import lax
from jax.sharding import PartitionSpec as P


def per_device(feats, tiles, tile_rows, tile_cols, tile_count, w_self, w_in, w_out, bias):
    tile_side = tiles.shape[-1]
    slot_count = tiles.shape[2]
    feat_width = feats.shape[1]
    node_block = feats.shape[0]
    rows_local = lax.axis_size("col") * node_block // tile_side
    cols_local = lax.axis_size("row") * node_block // tile_side
    own_tiles = tiles[0, 0]
    own_rows = tile_rows[0, 0]
    own_cols = tile_cols[0, 0]
    live_slots = jnp.arange(slot_count) < tile_count[0, 0]
    masked = jnp.where(live_slots[:, None, None], own_tiles, jnp.zeros_like(own_tiles))
    gathered = lax.all_gather(feats, "row", axis=0, tiled=True)
    picked = gathered.reshape(cols_local, tile_side, feat_width)[own_cols]
    products = jnp.einsum("sij,sjf->sif", masked, picked, preferred_element_type=jnp.float32)
    summed = jnp.zeros((rows_local, tile_side, feat_width), jnp.float32).at[own_rows].add(products)
    summed = summed.reshape(rows_local * tile_side, feat_width)
    inward_sum = lax.psum_scatter(
        summed.astype(jnp.bfloat16), "col", scatter_dimension=0, tiled=True
    )
    gathered = lax.all_gather(feats, "col", axis=0, tiled=True)
    picked = gathered.reshape(rows_local, tile_side, feat_width)[own_rows]
    products = jnp.einsum("sji,sjf->sif", masked, picked, preferred_element_type=jnp.float32)
    outward_summed = (
        jnp.zeros((cols_local, tile_side, feat_width), jnp.float32).at[own_cols].add(products)
    )
    outward_summed = outward_summed.reshape(cols_local * tile_side, feat_width)
    outward_sum = lax.psum_scatter(
        outward_summed.astype(jnp.bfloat16), "row", scatter_dimension=0, tiled=True
    )
    total = jnp.dot(feats, w_self, preferred_element_type=jnp.float32)
    total = total + jnp.dot(inward_sum, w_in, preferred_element_type=jnp.float32)
    total = total + jnp.dot(outward_sum, w_out, preferred_element_type=jnp.float32)
    total = total + bias[None, :]
    return jax.nn.relu(total).astype(jnp.bfloat16)


def solution(mesh):
    in_specs = (
        P(("row", "col"), None),
        P("row", "col", None, None, None),
        P("row", "col", None),
        P("row", "col", None),
        P("row", "col"),
        P(),
        P(),
        P(),
        P(),
    )
    out_specs = P(("row", "col"), None)
    return jax.shard_map(
        per_device, mesh=mesh, in_specs=in_specs, out_specs=out_specs, check_vma=False
    )
```

profile of v0, /device:TPU:16, one launch (start us, length us, event | category | flops | bytes accessed | tf_op | source)
XLA Modules:
  0.0 336.2 jit_solution(3296584931173622223)
XLA Ops:
  6.5 0.7 all-gather.3.cloned.1.call-update
  7.3 0.0 all-gather.5.cloned.1.call-start
  7.3 0.7 all-gather.5.cloned.1.call-update
  8.0 0.0 reduce-scatter.3.cloned.1.call-start
  8.7 0.7 fusion.6
  9.4 0.7 fusion.5
  10.0 65.2 %all-gather.3.cloned.1.call-done = bf16[4096,256]{1,0:T(8,128)(2,1)} async-done(((bf16[128,256]{1,0:T(8,128)(2,1)}), bf16[4096,256]{1,0:T(8,128)(2,1)}) %all-gather.3.cloned.1.call-update) | async-done | bytes 2097168 | tf_op jit(solution)/shard_map/all_gather | solution.py:19
  75.3 7.7 %gather_fusion = bf16[96,128,256]{2,1,0:T(8,128)(2,1)} fusion(bf16[32,128,256]{2,1,0:T(8,128)(2,1)} %bitcast.27, s32[1024]{0:T(1024)S(1)} %pad_clamp_fusion.1), kind=kCustom, calls=%fused_computation | custom fusion | bytes 12583296 | tf_op jit(solution)/shard_map/gather | solution.py:20
  83.0 9.2 %fusion.1 = f32[96,128,256]{2,1,0:T(8,128)} fusion(bf16[96,128,256]{2,1,0:T(8,128)(2,1)} %gather_fusion, bf16[1,1,96,128,128]{4,3,2,1,0:T(8,128)(2,1)S(1)} %copy-done.1, pred[96]{0:T(512)(128)(4,1)S(1)} %iota_compare_fusion), kind=kOutput, calls=%fused_computation.6 | convolution fusion | flops 806879232 | bytes 22020192 | tf_op jit(solution)/shard_map/sij,sjf->sif/dot_general | solution.py:21
  92.1 0.2 broadcast_in_dim.14
  92.3 18.4 %scatter_fusion = f32[16,128,256]{2,1,0:T(8,128)S(1)} fusion(f32[16,128,256]{2,1,0:T(8,128)S(1)} %broadcast_in_dim.14, s32[96]{0:T(128)S(1)} %fusion.5, f32[96,128,256]{2,1,0:T(8,128)} %fusion.1), kind=kCustom, calls=%fused_computation.2 | custom fusion | flops 3145728 | bytes 37749120 | tf_op jit(solution)/shard_map/scatter-add | solution.py:22
  110.7 1.1 convert_element_type.15
  111.8 0.0 reduce-scatter.5.cloned.1.call-start
  111.9 33.0 %all-gather.5.cloned.1.call-done = bf16[2048,256]{1,0:T(8,128)(2,1)} async-done(((bf16[128,256]{1,0:T(8,128)(2,1)}), bf16[2048,256]{1,0:T(8,128)(2,1)}) %all-gather.5.cloned.1.call-update) | async-done | bytes 1048592 | tf_op jit(solution)/shard_map/all_gather | solution.py:27
  144.9 7.3 %gather_fusion.1 = bf16[96,128,256]{2,1,0:T(8,128)(2,1)} fusion(bf16[16,128,256]{2,1,0:T(8,128)(2,1)} %bitcast.26, s32[1024]{0:T(1024)S(1)} %pad_clamp_fusion), kind=kCustom, calls=%fused_computation.1 | custom fusion | bytes 12583296 | tf_op jit(solution)/shard_map/gather | solution.py:28
  152.2 10.0 %fusion = f32[96,128,256]{2,1,0:T(8,128)} fusion(bf16[96,128,256]{2,1,0:T(8,128)(2,1)} %gather_fusion.1, bf16[1,1,96,128,128]{4,3,2,1,0:T(8,128)(2,1)S(1)} %copy-done.2, pred[96]{0:T(512)(128)(4,1)S(1)} %iota_compare_fusion), kind=kOutput, calls=%fused_computation.5 | convolution fusion | flops 806879232 | bytes 22020192 | tf_op jit(solution)/shard_map/sji,sjf->sif/dot_general | solution.py:29
  162.1 2.4 broadcast_in_dim.26
  164.6 28.6 %scatter_fusion.1 = f32[32,128,256]{2,1,0:T(8,128)} fusion(f32[32,128,256]{2,1,0:T(8,128)} %broadcast_in_dim.26, s32[96]{0:T(128)S(1)} %fusion.6, f32[96,128,256]{2,1,0:T(8,128)} %fusion), kind=kCustom, calls=%fused_computation.3 | custom fusion | flops 3145728 | bytes 37749120 | tf_op jit(solution)/shard_map/scatter-add | solution.py:31
  193.2 3.9 %convert_element_type.17 = bf16[32,128,256]{2,1,0:T(8,128)(2,1)} convert(f32[32,128,256]{2,1,0:T(8,128)} %scatter_fusion.1) | non-fusion elementwise | flops 1048576 | bytes 6291456 | tf_op jit(solution)/shard_map/convert_element_type | solution.py:35
  197.1 0.2 fusion.9
  197.3 23.4 %reduce-scatter.3.cloned.1.call-done = bf16[128,256]{1,0:T(8,128)(2,1)} async-done(((bf16[2048,256]{1,0:T(8,128)(2,1)}), bf16[128,256]{1,0:T(8,128)(2,1)}) %reduce-scatter.3.cloned.1.call-update) | async-done | bytes 65552 | tf_op jit(solution)/shard_map/reduce_scatter | solution.py:24
  220.6 1.0 convolution_add_fusion.1
  221.7 106.4 %reduce-scatter.5.cloned.1.call-done = bf16[128,256]{1,0:T(8,128)(2,1)} async-done(((bf16[4096,256]{1,0:T(8,128)(2,1)}), bf16[128,256]{1,0:T(8,128)(2,1)}) %reduce-scatter.5.cloned.1.call-update) | async-done | bytes 65552 | tf_op jit(solution)/shard_map/reduce_scatter | solution.py:34
  328.0 1.6 fusion.4
  (20 shorter events, 0.1 us)
Async XLA Ops:
  6.5 190.6 %copy-start = (bf16[256,256]{1,0:T(8,128)(2,1)S(1)}, bf16[256,256]{1,0:T(8,128)(2,1)}, u32[]{:S(2)}) copy-start(bf16[256,256]{1,0:T(8,128)(2,1)} %param.14) | copy-start | bytes 393220
  6.5 68.7 %all-gather.3.cloned.1.call-start = ((), (), s32[]{:S(2)}) async-start(), calls=%async_computation.2 | async-start | bytes 2162688 | tf_op jit(solution)/shard_map/all_gather | solution.py:19
  7.3 137.6 %all-gather.5.cloned.1.call-start = ((), (), s32[]{:S(2)}) async-start(), calls=%async_computation.4 | async-start | bytes 1114112 | tf_op jit(solution)/shard_map/all_gather | solution.py:27
  8.0 212.6 %reduce-scatter.3.cloned.1.call-start = ((), (), s32[]{:S(2)}) async-start(), calls=%async_computation.3 | async-start | bytes 1114112 | tf_op jit(solution)/shard_map/reduce_scatter | solution.py:24
  75.3 7.7 %copy-start.1 = (bf16[1,1,96,128,128]{4,3,2,1,0:T(8,128)(2,1)S(1)}, bf16[1,1,96,128,128]{4,3,2,1,0:T(8,128)(2,1)}, u32[]{:S(2)}) copy-start(bf16[1,1,96,128,128]{4,3,2,1,0:T(8,128)(2,1)} %param.10) | copy-start | bytes 9437188
  111.8 216.2 %reduce-scatter.5.cloned.1.call-start = ((), (), s32[]{:S(2)}) async-start(), calls=%async_computation.5 | async-start | bytes 2162688 | tf_op jit(solution)/shard_map/reduce_scatter | solution.py:34
  144.9 7.3 %copy-start.2 = (bf16[1,1,96,128,128]{4,3,2,1,0:T(8,128)(2,1)S(1)}, bf16[1,1,96,128,128]{4,3,2,1,0:T(8,128)(2,1)}, u32[]{:S(2)}) copy-start(bf16[1,1,96,128,128]{4,3,2,1,0:T(8,128)(2,1)} %param.10) | copy-start | bytes 9437188
  193.2 3.9 %copy-start.3 = (bf16[128,256]{1,0:T(8,128)(2,1)S(1)}, bf16[128,256]{1,0:T(8,128)(2,1)}, u32[]{:S(2)}) copy-start(bf16[128,256]{1,0:T(8,128)(2,1)} %param.9) | copy-start | bytes 196612
  193.2 27.5 %copy-start.4 = (bf16[256,256]{1,0:T(8,128)(2,1)S(1)}, bf16[256,256]{1,0:T(8,128)(2,1)}, u32[]{:S(2)}) copy-start(bf16[256,256]{1,0:T(8,128)(2,1)} %param.15) | copy-start | bytes 393220
  193.2 134.8 %copy-start.5 = (bf16[256,256]{1,0:T(8,128)(2,1)S(1)}, bf16[256,256]{1,0:T(8,128)(2,1)}, u32[]{:S(2)}) copy-start(bf16[256,256]{1,0:T(8,128)(2,1)} %param.16) | copy-start | bytes 393220
  193.2 134.8 %copy-start.6 = (f32[256]{0:T(256)S(1)}, f32[256]{0:T(256)}, u32[]{:S(2)}) copy-start(f32[256]{0:T(256)} %param.17) | copy-start | bytes 3076
Sparse Core Ops, SparseCore 0:
  10.5 64.7 all-gather.2
  77.3 67.4 all-gather.4
  147.7 72.9 reduce-scatter.2
  225.6 102.4 reduce-scatter.4
where the time goes:
time: 337 us; the launch traced here: 336 us
  waiting for transfers between devices  229 us (68%)
  other arithmetic  53.3 us (16%)
  matrix products  21.9 us (6%)
  local copies, waits for them, and re-layouts  17.6 us (5%)
  between operations  13.8 us (4%)
    reduce_scatter x1, waiting for transfers between devices, per_device(): lax.psum_scatter(outward_summed.astype(jnp.bfloat16), 'row', scatter_dime...  106 us
    all_gather x1, waiting for transfers between devices, per_device(): gathered = lax.all_gather(feats, 'row', axis=0, tiled=True)  65.2 us
    all_gather x1, waiting for transfers between devices, per_device(): gathered = lax.all_gather(feats, 'col', axis=0, tiled=True)  33 us
    scatter-add x1, other arithmetic, per_device(): jnp.zeros((cols_local, tile_side, feat_width), jnp.float32).at[own_cols]  28.6 us
    reduce_scatter x1, waiting for transfers between devices, per_device(): lax.psum_scatter(summed.astype(jnp.bfloat16), 'col', scatter_dimension=0,...  23.4 us
    scatter-add x1, other arithmetic, per_device(): jnp.zeros((rows_local, tile_side, feat_width), jnp.float32).at[own_rows]  18.4 us
    dot_general x1, matrix products, per_device(): jnp.einsum('sji,sjf->sif', masked, picked, preferred_element_type=jnp.flo...  9.97 us
    dot_general x1, matrix products, per_device(): jnp.einsum('sij,sjf->sif', masked, picked, preferred_element_type=jnp.flo...  9.16 us
  transfers between devices with their start and end apart: 4, of which 4 were waited for; matrix products, arithmetic and copies ran while one was open for 27% of the time, Pallas kernels for 0%

commit v1 on v0

v1 whole, which is shorter than its diff:
```python
import functools

import jax
import jax.numpy as jnp
from jax import lax
from jax.experimental import pallas as pl
from jax.experimental.pallas import tpu as pltpu
from jax.sharding import Mesh, PartitionSpec as P

ZH, X, CORE, Y, ZL = "zh", "x", "core", "y", "zl"
UNROLL = 8
VMEM_LIMIT = 40 * 2**20


def group_loop(count, body):
    lax.fori_loop(0, lax.div(count + (UNROLL - 1), UNROLL), lambda g, _: (body(g), 0)[1], 0)


def outward_kernel(scalars, rows, cols, tiles, panel, keep, send, acc):
    acc[...] = jnp.zeros_like(acc)
    count, core = scalars[0], scalars[1]

    def body(group):
        products = []
        for step in range(UNROLL):
            slot = group * UNROLL + step
            tile = jnp.where(slot < count, tiles[slot], jnp.zeros((), tiles.dtype))
            product = lax.dot_general(
                tile, panel[rows[slot]], (((0,), (0,)), ((), ())), preferred_element_type=jnp.float32
            )
            col = cols[slot]
            products.append(((((col & 1) ^ core) * 16) + (col >> 1), product))
        for place, product in products:
            acc[place] += product

    group_loop(count, body)
    keep[...] = acc[:16].astype(keep.dtype)
    send[...] = acc[16:].astype(send.dtype)


def inward_kernel(scalars, rows, cols, tiles, panel, out, acc):
    acc[...] = jnp.zeros_like(acc)
    count = scalars[0]

    def body(group):
        products = []
        for step in range(UNROLL):
            slot = group * UNROLL + step
            tile = jnp.where(slot < count, tiles[slot], jnp.zeros((), tiles.dtype))
            col = cols[slot]
            product = jnp.dot(
                tile, panel[(col & 1) * 16 + (col >> 1)], preferred_element_type=jnp.float32
            )
            products.append((rows[slot], product))
        for place, product in products:
            acc[place] += product

    group_loop(count, body)
    out[...] = acc[...].astype(out.dtype)


def final_kernel(feats, terms_in, terms_out, w_self, w_in, w_out, bias, out):
    def summed(terms):
        total = terms[0].astype(jnp.float32)
        for k in range(1, terms.shape[0]):
            total = total + terms[k].astype(jnp.float32)
        return total.astype(jnp.bfloat16)

    total = jnp.dot(feats[...], w_self[...], preferred_element_type=jnp.float32)
    total = total + jnp.dot(summed(terms_in), w_in[...], preferred_element_type=jnp.float32)
    total = total + jnp.dot(summed(terms_out), w_out[...], preferred_element_type=jnp.float32)
    out[...] = jnp.maximum(total + bias[...], 0.0).astype(out.dtype)


SMEM = pl.BlockSpec(memory_space=pltpu.SMEM)
VMEM = pl.BlockSpec(memory_space=pltpu.VMEM)


def spmm_call(kernel, outs, acc_tiles, scalars, rows, cols, tiles, panel):
    side, width = tiles.shape[-1], panel.shape[-1]
    return pl.pallas_call(
        kernel,
        out_shape=[jax.ShapeDtypeStruct((n, side, width), jnp.bfloat16) for n in outs],
        in_specs=[SMEM] * 3 + [VMEM] * 2,
        out_specs=[VMEM] * len(outs),
        scratch_shapes=[pltpu.VMEM((acc_tiles, side, width), jnp.float32)],
        compiler_params=pltpu.CompilerParams(vmem_limit_bytes=VMEM_LIMIT),
        cost_estimate=pl.CostEstimate(
            flops=2 * tiles.shape[0] * side * side * width,
            bytes_accessed=8 * 2**20,
            transcendentals=0,
        ),
    )(scalars, rows, cols, tiles, panel)


def exchange(parts, axes):
    return lax.all_to_all(parts, axes, 0, 0, tiled=True)


def per_device(feats, tiles, tile_rows, tile_cols, tile_count, w_self, w_in, w_out, bias):
    tiles, rows, cols = tiles[0, 0], tile_rows[0, 0], tile_cols[0, 0]
    core = lax.axis_index(CORE)
    scalars = jnp.stack([tile_count[0, 0], core.astype(jnp.int32)])
    side, width = feats.shape
    row_panel = lax.all_gather(lax.all_gather(feats, ZL), Y).reshape(16, side, width)
    col_panel = exchange(jnp.broadcast_to(feats[None], (16, side, width)), (ZH, X))
    col_panel = lax.all_gather(col_panel, CORE).reshape(32, side, width)
    keep, send = spmm_call(outward_kernel, (16, 16), 32, scalars, rows, cols, tiles, row_panel)
    got = lax.ppermute(send, CORE, [(0, 1), (1, 0)])
    (terms_in,) = spmm_call(inward_kernel, (16,), 16, scalars, rows, cols, tiles, col_panel)
    pair = (keep.astype(jnp.float32) + got.astype(jnp.float32)).astype(jnp.bfloat16)
    terms_out = exchange(pair, (ZH, X))
    terms_in = exchange(terms_in, (Y, ZL))
    return pl.pallas_call(
        final_kernel,
        out_shape=jax.ShapeDtypeStruct((side, width), jnp.bfloat16),
        in_specs=[VMEM] * 7,
        out_specs=VMEM,
        compiler_params=pltpu.CompilerParams(vmem_limit_bytes=VMEM_LIMIT),
    )(feats, terms_in, terms_out, w_self, w_in, w_out, bias[None, :])


def solution(mesh):
    split = Mesh(mesh.devices.reshape(4, 4, 2, 8, 2), (ZH, X, CORE, Y, ZL))
    row, col = (ZH, X, CORE), (Y, ZL)
    in_specs = (
        P(row + col, None),
        P(row, col, None, None, None),
        P(row, col, None),
        P(row, col, None),
        P(row, col),
        P(),
        P(),
        P(),
        P(),
    )
    return jax.shard_map(
        per_device, mesh=split, in_specs=in_specs, out_specs=P(row + col, None), check_vma=False
    )
```

time: 337 us -> 158 us (0.47)
  the two profiles are of different devices: /device:TPU:16 before, /device:TPU:2 now
where the time goes in v1:
time: 158 us
  waiting for transfers between devices  57.1 us (36%)
  blocking collectives  42.6 us (27%)
  starting transfers between devices  26 us (16%)
  between operations  15.6 us (10%)
  Pallas kernels  6.9 us (4%)
  local copies, waits for them, and re-layouts  6.75 us (4%)
  other arithmetic  2.9 us (2%)
    all_to_all x1, blocking collectives, exchange(): return lax.all_to_all(parts, axes, 0, 0, tiled=True)  35.3 us
    all_gather x1, waiting for transfers between devices, per_device(): lax.all_gather(lax.all_gather(feats, ZL), Y).reshape(16, side, width)  29.7 us
    all_to_all x2, starting transfers between devices, exchange(): return lax.all_to_all(parts, axes, 0, 0, tiled=True)  24.1 us
    all_to_all x2, waiting for transfers between devices, exchange(): return lax.all_to_all(parts, axes, 0, 0, tiled=True)  21.1 us
    all_gather x1, blocking collectives, per_device(): lax.all_gather(feats, ZL)  7.36 us
    unnamed x24, local copies, waits for them, and re-layouts  4.82 us
    pallas_call x2, Pallas kernels, spmm_call(): pl.pallas_call(kernel, out_shape=[jax.ShapeDtypeStruct((n, side, width),...  4.61 us
    all_gather x1, waiting for transfers between devices, per_device(): col_panel = lax.all_gather(col_panel, CORE).reshape(32, side, width)  3.33 us
  transfers between devices with their start and end apart: 5, of which 4 were waited for; matrix products, arithmetic and copies ran while one was open for 3% of the time, Pallas kernels for 3%

profile of v1, /device:TPU:2, one launch (start us, length us, event | category | flops | bytes accessed | tf_op | source)
XLA Modules:
  0.0 157.9 jit_solution(6701046048645071559)
XLA Ops:
  7.4 7.4 %all-gather.1 = bf16[256,256]{1,0:T(8,128)(2,1)} all-gather(bf16[128,256]{1,0:T(8,128)(2,1)} %feats.1), channel_id=3, replica_groups=mesh['zh'=4,'x'=4,'core'=2,'y'=8,'zl'=2] {'zl'}, dimensions={0}, use_global_device_ids=true | all-gather | bytes 196608 | tf_op jit(solution)/shard_map/all_gather | solution.py:105
  14.7 0.0 all-gather.8.cloned.1.call-update
  14.8 1.9 %broadcast_in_dim.11 = bf16[16,128,256]{2,1,0:T(8,128)(2,1)} broadcast(bf16[128,256]{1,0:T(8,128)(2,1)} %feats.1), dimensions={1,2} | broadcast | bytes 1114112 | tf_op jit(solution)/shard_map/broadcast_in_dim | solution.py:106
  16.7 12.4 %all-to-all-start = ((bf16[16,128,256]{2,1,0:T(8,128)(2,1)}), bf16[16,128,256]{2,1,0:T(8,128)(2,1)}, u32[]{:S(2)}, u32[]{:S(2)}) async-start(bf16[16,128,256]{2,1,0:T(8,128)(2,1)} %broadcast_in_dim.11), calls=%async_computation | async-start | bytes 2097152 | tf_op jit(solution)/shard_map/all_to_all | solution.py:97
  29.1 0.0 all-gather.6.cloned.1.call-start
  29.8 0.1 pad_add_fusion.scalars
  29.9 29.7 %all-gather.8.cloned.1.call-done.panel = bf16[16,128,256]{2,1,0:T(8,128)(2,1)} async-done(((bf16[2,128,256]{2,1,0:T(8,128)(2,1)}), bf16[16,128,256]{2,1,0:T(8,128)(2,1)}) %all-gather.8.cloned.1.call-update) | async-done | bytes 1048592 | tf_op jit(solution)/shard_map/all_gather | solution.py:105
  59.6 1.2 copy-done.3
  60.8 2.9 %shard_map.92 = (bf16[16,128,256]{2,1,0:T(8,128)(2,1)S(1)}, bf16[16,128,256]{2,1,0:T(8,128)(2,1)}) custom-call(s32[2]{0:T(128)S(1)} %pad_add_fusion.scalars, s32[96]{0:T(128)S(1)} %bitcast.10, s32[96]{0:T(128)S(1)} %bitcast.12, bf16[96,128,128]{2,1,0:T(8,128)(2,1)S(1)} %bitcast.8, bf16[16,128,256]{2,1,0:T(8,128)(2,1)S(1)} %copy-done.3), custom_call_target="tpu_custom_call" | custom-call | flops 805306368 | bytes 8388608 | tf_op jit(solution)/shard_map/pallas_call | solution.py:81
  63.7 1.0 copy-done.4
  64.7 1.9 %collective-permute-start = (bf16[16,128,256]{2,1,0:T(8,128)(2,1)}, bf16[16,128,256]{2,1,0:T(8,128)(2,1)}, u32[]{:S(2)}, u32[]{:S(2)}) collective-permute-start(bf16[16,128,256]{2,1,0:T(8,128)(2,1)} %get-tuple-element.8), channel_id=1, source_target_pairs={{0,16},{16,0},{1,17},{17,1},{2,18},{18,2},{3,19},{19,3},{4,20},{20... | collective-permute-start | bytes 3145736 | tf_op jit(solution)/shard_map/ppermute | solution.py:109
  66.6 0.0 all-to-all-done
  66.6 0.0 all-gather.6.cloned.1.call-update
  66.6 2.9 %collective-permute-done = bf16[16,128,256]{2,1,0:T(8,128)(2,1)} collective-permute-done((bf16[16,128,256]{2,1,0:T(8,128)(2,1)}, bf16[16,128,256]{2,1,0:T(8,128)(2,1)}, u32[]{:S(2)}, u32[]{:S(2)}) %collective-permute-start) | collective-permute-done | bytes 1048608 | tf_op jit(solution)/shard_map/ppermute | solution.py:109
  69.6 2.8 %add_convert_fusion = bf16[16,128,256]{2,1,0:T(8,128)(2,1)} fusion(bf16[16,128,256]{2,1,0:T(8,128)(2,1)} %collective-permute-done, bf16[16,128,256]{2,1,0:T(8,128)(2,1)} %copy-done.4), kind=kLoop, calls=%fused_computation | loop fusion | flops 2097152 | bytes 3145728 | tf_op jit(solution)/shard_map/convert_element_type | solution.py:111
  72.4 11.7 %all-to-all-start.2 = ((bf16[16,128,256]{2,1,0:T(8,128)(2,1)}), bf16[16,128,256]{2,1,0:T(8,128)(2,1)}, u32[]{:S(2)}, u32[]{:S(2)}) async-start(bf16[16,128,256]{2,1,0:T(8,128)(2,1)} %add_convert_fusion), calls=%async_computation.2 | async-start | bytes 2097152 | tf_op jit(solution)/shard_map/all_to_all | solution.py:97
  84.1 3.3 %all-gather.6.cloned.1.call-done.panel = bf16[32,128,256]{2,1,0:T(8,128)(2,1)} async-done(((bf16[16,128,256]{2,1,0:T(8,128)(2,1)}), bf16[32,128,256]{2,1,0:T(8,128)(2,1)}) %all-gather.6.cloned.1.call-update) | async-done | bytes 2097168 | tf_op jit(solution)/shard_map/all_gather | solution.py:107
  87.4 1.6 %copy-done.2 = bf16[32,128,256]{2,1,0:T(8,128)(2,1)S(1)} copy-done((bf16[32,128,256]{2,1,0:T(8,128)(2,1)S(1)}, bf16[32,128,256]{2,1,0:T(8,128)(2,1)}, u32[]{:S(2)}) %copy-start.2) | copy-done | bytes 2097176
  89.0 1.7 %shard_map.91 = bf16[16,128,256]{2,1,0:T(8,128)(2,1)S(1)} custom-call(s32[2]{0:T(128)S(1)} %pad_add_fusion.scalars, s32[96]{0:T(128)S(1)} %bitcast.11, s32[96]{0:T(128)S(1)} %bitcast.13, bf16[96,128,128]{2,1,0:T(8,128)(2,1)S(1)} %bitcast.9, bf16[32,128,256]{2,1,0:T(8,128)(2,1)S(1)} %copy-done.2), custom_call_target="tpu_custom_call" | custom-call | flops 805306368 | bytes 8388608 | tf_op jit(solution)/shard_map/pallas_call | solution.py:81
  90.7 1.0 copy-done.1
  91.7 0.0 copy-start.11
  91.7 21.1 %all-to-all-done.2.terms_out = bf16[16,128,256]{2,1,0:T(8,128)(2,1)} async-done(((bf16[16,128,256]{2,1,0:T(8,128)(2,1)}), bf16[16,128,256]{2,1,0:T(8,128)(2,1)}, u32[]{:S(2)}, u32[]{:S(2)}) %all-to-all-start.2) | async-done | bytes 1048608 | tf_op jit(solution)/shard_map/all_to_all | solution.py:97
  112.8 35.3 %all_to_all.15.terms_in = bf16[16,128,256]{2,1,0:T(8,128)(2,1)S(1)} all-to-all(bf16[16,128,256]{2,1,0:T(8,128)(2,1)} %copy-done.1), channel_id=1, replica_groups=mesh['zh'=4,'x'=4,'core'=2,'y'=8,'zl'=2] {'y','zl'}, dimensions={0} | all-to-all | bytes 2097152 | tf_op jit(solution)/shard_map/all_to_all | solution.py:97
  148.2 2.3 %shard_map.93 = bf16[128,256]{1,0:T(8,128)(2,1)} custom-call(bf16[128,256]{1,0:T(8,128)(2,1)S(1)} %copy-done.5, bf16[16,128,256]{2,1,0:T(8,128)(2,1)S(1)} %all_to_all.15.terms_in, bf16[16,128,256]{2,1,0:T(8,128)(2,1)} %all-to-all-done.2.terms_out, bf16[256,256]{1,0:T(8,128)(2,1)S(1)} %copy-done.6, bf16[256,256]{1,0:T(8,128)(2,1)S(1)} %copy-done.7, ...), custom_call_target="tpu_custom_call" | custom-call | tf_op jit(solution)/shard_map/pallas_call | solution.py:114
  (20 shorter events, 0.0 us)
Async XLA Ops:
  7.4 52.2 %copy-start.9 = (s32[1,1,96]{2,1,0:T(1,128)S(1)}, s32[1,1,96]{2,1,0:T(1,128)}, u32[]{:S(2)}) copy-start(s32[1,1,96]{2,1,0:T(1,128)} %param.11) | copy-start | bytes 1156
  7.4 52.2 %copy-start.10 = (s32[1,1,96]{2,1,0:T(1,128)S(1)}, s32[1,1,96]{2,1,0:T(1,128)}, u32[]{:S(2)}) copy-start(s32[1,1,96]{2,1,0:T(1,128)} %param.12) | copy-start | bytes 1156
  7.4 52.2 %copy-start = (bf16[1,1,96,128,128]{4,3,2,1,0:T(8,128)(2,1)S(1)}, bf16[1,1,96,128,128]{4,3,2,1,0:T(8,128)(2,1)}, u32[]{:S(2)}) copy-start(bf16[1,1,96,128,128]{4,3,2,1,0:T(8,128)(2,1)} %param.10) | copy-start | bytes 9437188
  7.4 52.2 %all-gather.8.cloned.1.call-start = ((), (), s32[]{:S(2)}) async-start(), calls=%async_computation.4 | async-start | bytes 1179648 | tf_op jit(solution)/shard_map/all_gather | solution.py:105
  16.7 49.9 %all-to-all-start = ((bf16[16,128,256]{2,1,0:T(8,128)(2,1)}), bf16[16,128,256]{2,1,0:T(8,128)(2,1)}, u32[]{:S(2)}, u32[]{:S(2)}) async-start(bf16[16,128,256]{2,1,0:T(8,128)(2,1)} %broadcast_in_dim.11), calls=%async_computation | async-start | bytes 2097152 | tf_op jit(solution)/shard_map/all_to_all | solution.py:97
  29.1 58.3 %all-gather.6.cloned.1.call-start = ((), (), s32[]{:S(2)}) async-start(), calls=%async_computation.3 | async-start | bytes 3145728 | tf_op jit(solution)/shard_map/all_gather | solution.py:107
  59.6 1.2 copy-start.3
  63.7 1.0 copy-start.4
  64.7 4.9 %collective-permute-start = (bf16[16,128,256]{2,1,0:T(8,128)(2,1)}, bf16[16,128,256]{2,1,0:T(8,128)(2,1)}, u32[]{:S(2)}, u32[]{:S(2)}) collective-permute-start(bf16[16,128,256]{2,1,0:T(8,128)(2,1)} %get-tuple-element.8), channel_id=1, source_target_pairs={{0,16},{16,0},{1,17},{17,1},{2,18},{18,2},{3,19},{19,3},{4,20},{20... | collective-permute-start | bytes 3145736 | tf_op jit(solution)/shard_map/ppermute | solution.py:109
  72.4 40.4 %all-to-all-start.2 = ((bf16[16,128,256]{2,1,0:T(8,128)(2,1)}), bf16[16,128,256]{2,1,0:T(8,128)(2,1)}, u32[]{:S(2)}, u32[]{:S(2)}) async-start(bf16[16,128,256]{2,1,0:T(8,128)(2,1)} %add_convert_fusion), calls=%async_computation.2 | async-start | bytes 2097152 | tf_op jit(solution)/shard_map/all_to_all | solution.py:97
  87.4 1.6 %copy-start.2 = (bf16[32,128,256]{2,1,0:T(8,128)(2,1)S(1)}, bf16[32,128,256]{2,1,0:T(8,128)(2,1)}, u32[]{:S(2)}) copy-start(bf16[32,128,256]{2,1,0:T(8,128)(2,1)} %all-gather.6.cloned.1.call-done.panel) | copy-start | bytes 6291460
  90.7 1.0 copy-start.1
  91.7 56.4 %copy-start.5 = (bf16[128,256]{1,0:T(8,128)(2,1)S(1)}, bf16[128,256]{1,0:T(8,128)(2,1)}, u32[]{:S(2)}) copy-start(bf16[128,256]{1,0:T(8,128)(2,1)} %feats.1) | copy-start | bytes 196612
  91.7 56.4 %copy-start.6 = (bf16[256,256]{1,0:T(8,128)(2,1)S(1)}, bf16[256,256]{1,0:T(8,128)(2,1)}, u32[]{:S(2)}) copy-start(bf16[256,256]{1,0:T(8,128)(2,1)} %w_self.1) | copy-start | bytes 393220
  91.7 56.4 %copy-start.7 = (bf16[256,256]{1,0:T(8,128)(2,1)S(1)}, bf16[256,256]{1,0:T(8,128)(2,1)}, u32[]{:S(2)}) copy-start(bf16[256,256]{1,0:T(8,128)(2,1)} %w_in.1) | copy-start | bytes 393220
  91.7 56.4 %copy-start.8 = (bf16[256,256]{1,0:T(8,128)(2,1)S(1)}, bf16[256,256]{1,0:T(8,128)(2,1)}, u32[]{:S(2)}) copy-start(bf16[256,256]{1,0:T(8,128)(2,1)} %w_out.1) | copy-start | bytes 393220
  91.7 56.5 %copy-start.11 = (f32[256]{0:T(256)S(1)}, f32[256]{0:T(256)}, u32[]{:S(2)}) copy-start(f32[256]{0:T(256)} %param.17) | copy-start | bytes 3076
Sparse Core Ops, SparseCore 0:
  14.9 44.6 all-gather.7
Sparse Core Ops, SparseCore 1:
  66.7 20.6 all-gather.5

commit v2 on v1

v2 whole, which is shorter than its diff:
```python
import functools

import jax
import jax.numpy as jnp
from jax import lax
from jax.experimental import pallas as pl
from jax.experimental.pallas import tpu as pltpu
from jax.sharding import Mesh, PartitionSpec as P

ZH, X, CORE, Y, ZL = "zh", "x", "core", "y", "zl"
UNROLL = 8
VMEM_LIMIT = 20 * 2**20
SMEM = pl.BlockSpec(memory_space=pltpu.SMEM)
VMEM = pl.BlockSpec(memory_space=pltpu.VMEM)
ANY = pl.BlockSpec(memory_space=pl.ANY)


def panel_place(block, own_zl):
    return (((block & 1) ^ own_zl) << 3) | (block >> 1)


def col_place(block, own_zl):
    return block ^ own_zl


def pair_place(block, core):
    return (((block & 1) ^ core) << 4) | (block >> 1)


def row_place(block, core, own_x):
    return (((block & 1) ^ core) << 4) | ((((block >> 1) & 3) ^ own_x) << 2) | (block >> 3)


def walk_slots(count, tiles, product, acc):
    acc[...] = jnp.zeros_like(acc)

    def body(group, _):
        done = []
        for step in range(UNROLL):
            slot = group * UNROLL + step
            tile = jnp.where(slot < count, tiles[slot], jnp.zeros((), tiles.dtype))
            done.append(product(slot, tile))
        for place, value in done:
            acc[place] += value
        return 0

    lax.fori_loop(0, lax.div(count + (UNROLL - 1), UNROLL), body, 0)


def fill(panel, parts):
    start = 0
    for part in parts:
        panel[start : start + part.shape[0]] = part[...]
        start += part.shape[0]


def outward_kernel(parts, scalars, rows, cols, tiles, *refs):
    keep, send, panel, acc = refs[-4:]
    fill(panel, refs[:parts])
    core, own_zl, own_x = scalars[1], scalars[2], scalars[3]

    def product(slot, tile):
        value = lax.dot_general(
            tile,
            panel[panel_place(rows[slot], own_zl)],
            (((0,), (0,)), ((), ())),
            preferred_element_type=jnp.float32,
        )
        return row_place(cols[slot], core, own_x), value

    walk_slots(scalars[0], tiles, product, acc)
    keep[...] = acc[:16].astype(keep.dtype)
    send[...] = acc[16:].astype(send.dtype)


def inward_kernel(parts, scalars, rows, cols, tiles, *refs):
    out, panel, acc = refs[-3:]
    fill(panel, refs[:parts])
    core, own_zl = scalars[1], scalars[2]

    def product(slot, tile):
        value = jnp.dot(
            tile, panel[pair_place(cols[slot], core)], preferred_element_type=jnp.float32
        )
        return col_place(rows[slot], own_zl), value

    walk_slots(scalars[0], tiles, product, acc)
    out[...] = acc[...].astype(out.dtype)


def add_kernel(terms, pieces, *refs):
    outs = refs[len(refs) - pieces :]
    size = outs[0].shape[0]
    for k, out in enumerate(outs):
        part = pl.ds(k * size, size)
        total = refs[0][part].astype(jnp.float32)
        for ref in refs[1:terms]:
            total = total + ref[part].astype(jnp.float32)
        out[...] = total.astype(out.dtype)


def final_kernel(feats, w_self, w_in, w_out, bias, terms_out, *refs):
    *terms_in, out = refs

    def product(terms, weight):
        total = terms[0].astype(jnp.float32)
        for term in terms[1:]:
            total = total + term.astype(jnp.float32)
        return jnp.dot(
            total.astype(jnp.bfloat16), weight[...], preferred_element_type=jnp.float32
        )

    total = jnp.dot(feats[...], w_self[...], preferred_element_type=jnp.float32)
    total = total + product([term[0] for term in terms_in], w_in)
    total = total + product([terms_out[k] for k in range(terms_out.shape[0])], w_out)
    out[...] = jnp.maximum(total + bias[...], 0.0).astype(out.dtype)


def copies_kernel(value, *refs):
    out = refs[-1]
    size = value.shape[0]
    for k in range(out.shape[0] // size):
        out[k * size : (k + 1) * size] = value[...]


def copies_call(value, count, after=()):
    return pl.pallas_call(
        copies_kernel,
        out_shape=jax.ShapeDtypeStruct((count * value.shape[0], *value.shape[1:]), value.dtype),
        in_specs=[VMEM] * (1 + len(after)),
        out_specs=VMEM,
        compiler_params=pltpu.CompilerParams(vmem_limit_bytes=VMEM_LIMIT),
        cost_estimate=pl.CostEstimate(
            flops=0, bytes_accessed=2 * (count + 1) * value.size, transcendentals=0
        ),
    )(value, *after)


def tie_kernel(*refs):
    pass


def tie_call(value, *after):
    return pl.pallas_call(
        tie_kernel,
        out_shape=jax.ShapeDtypeStruct(value.shape, value.dtype),
        in_specs=[ANY] * (1 + len(after)),
        out_specs=ANY,
        input_output_aliases={0: 0},
    )(value, *after)


def fold_kernel(parts, *outs):
    for k, out in enumerate(outs):
        total = parts[k].astype(jnp.float32)
        for start in range(len(outs), parts.shape[0], len(outs)):
            total = total + parts[start + k].astype(jnp.float32)
        out[...] = total[None].astype(out.dtype)


def fold_call(parts, pieces):
    shape = jax.ShapeDtypeStruct((1, *parts.shape[1:]), parts.dtype)
    return pl.pallas_call(
        fold_kernel,
        out_shape=[shape] * pieces,
        in_specs=[VMEM],
        out_specs=[VMEM] * pieces,
        compiler_params=pltpu.CompilerParams(vmem_limit_bytes=VMEM_LIMIT),
        cost_estimate=pl.CostEstimate(
            flops=parts.size, bytes_accessed=3 * parts.size, transcendentals=0
        ),
    )(parts)


def spmm_call(kernel, outs, out_tiles, panel_tiles, scalars, rows, cols, tiles, parts, after=()):
    side, width = tiles.shape[-1], parts[0].shape[-1]
    return pl.pallas_call(
        functools.partial(kernel, len(parts)),
        out_shape=[jax.ShapeDtypeStruct((out_tiles // outs, side, width), jnp.bfloat16)] * outs,
        in_specs=[SMEM] * 3 + [VMEM] * (1 + len(parts) + len(after)),
        out_specs=[VMEM] * outs,
        scratch_shapes=[
            pltpu.VMEM((panel_tiles, side, width), jnp.bfloat16),
            pltpu.VMEM((out_tiles, side, width), jnp.float32),
        ],
        compiler_params=pltpu.CompilerParams(vmem_limit_bytes=VMEM_LIMIT),
        cost_estimate=pl.CostEstimate(
            flops=2 * tiles.shape[0] * side * side * width,
            bytes_accessed=8 * 2**20,
            transcendentals=0,
        ),
    )(scalars, rows, cols, tiles, *parts, *after)


def add_call(terms, pieces, after=()):
    count, side, width = terms[0].shape
    size = terms[0].size
    return pl.pallas_call(
        functools.partial(add_kernel, len(terms), pieces),
        out_shape=[jax.ShapeDtypeStruct((count // pieces, side, width), jnp.bfloat16)] * pieces,
        in_specs=[VMEM] * (len(terms) + len(after)),
        out_specs=[VMEM] * pieces,
        compiler_params=pltpu.CompilerParams(vmem_limit_bytes=VMEM_LIMIT),
        cost_estimate=pl.CostEstimate(
            flops=size * len(terms), bytes_accessed=2 * size * (len(terms) + 1), transcendentals=0
        ),
    )(*terms, *after)


def exchange(parts, axis):
    return lax.all_to_all(parts, axis, 0, 0, tiled=True)


def swap(value, axis, bit):
    size = lax.axis_size(axis)
    return lax.ppermute(value, axis, [(i, i ^ bit) for i in range(size)])


def per_device(feats, tiles, tile_rows, tile_cols, tile_count, w_self, w_in, w_out, bias):
    tiles, rows, cols = tiles[0, 0], tile_rows[0, 0], tile_cols[0, 0]
    side, width = feats.shape
    scalars = jnp.stack(
        [tile_count[0, 0], lax.axis_index(CORE), lax.axis_index(ZL), lax.axis_index(X)]
    ).astype(jnp.int32)

    near_col = exchange(copies_call(feats[None], 16), (ZH, X))
    near_row = lax.all_gather(feats, Y)
    far_row = swap(near_row, ZL, 1)
    near_col = tie_call(near_col, near_row)
    far_col = swap(near_col, CORE, 1)

    (inward,) = spmm_call(
        inward_kernel, 1, 16, 32, scalars, rows, cols, tiles, (near_col, far_col)
    )
    keep_out, send_out = spmm_call(
        outward_kernel, 2, 32, 16, scalars, rows, cols, tiles, (near_row, far_row), (inward,)
    )
    inward = exchange(inward, Y)
    parts = add_call([keep_out, swap(send_out, CORE, 1)], 4)
    got = [swap(part, X, bit) for part, bit in zip(parts[1:], (1, 2, 3))]
    (outward,) = add_call([parts[0], *got], 1)
    terms_out = exchange(outward, ZH)
    keep, send = fold_call(inward, 2)
    terms_in = [keep, swap(send, ZL, 1)]
    return pl.pallas_call(
        final_kernel,
        out_shape=jax.ShapeDtypeStruct((side, width), jnp.bfloat16),
        in_specs=[VMEM] * 8,
        out_specs=VMEM,
        compiler_params=pltpu.CompilerParams(vmem_limit_bytes=VMEM_LIMIT),
    )(feats, w_self, w_in, w_out, bias[None, :], terms_out, *terms_in)


def solution(mesh):
    split = Mesh(mesh.devices.reshape(4, 4, 2, 8, 2), (ZH, X, CORE, Y, ZL))
    row, col = (ZH, X, CORE), (Y, ZL)
    in_specs = (
        P(row + col, None),
        P(row, col, None, None, None),
        P(row, col, None),
        P(row, col, None),
        P(row, col),
        P(),
        P(),
        P(),
        P(),
    )
    return jax.shard_map(
        per_device, mesh=split, in_specs=in_specs, out_specs=P(row + col, None), check_vma=False
    )
```

time: 158 us -> 119 us (0.75)
  the two profiles are of different devices: /device:TPU:2 before, /device:TPU:16 now
where the time goes in v2:
time: 119 us
  starting transfers between devices  49.4 us (42%)
  blocking collectives  28.5 us (24%)
  waiting for transfers between devices  23.9 us (20%)
  Pallas kernels  10.7 us (9%)
  local copies, waits for them, and re-layouts  5.1 us (4%)
    all_gather x1, blocking collectives, per_device(): near_row = lax.all_gather(feats, Y)  28.5 us
    all_to_all x3, starting transfers between devices, exchange(): return lax.all_to_all(parts, axis, 0, 0, tiled=True)  26 us
    ppermute x7, starting transfers between devices, swap(): return lax.ppermute(value, axis, [(i, i ^ bit) for i in range(size)])  23.5 us
    ppermute x7, waiting for transfers between devices, swap(): return lax.ppermute(value, axis, [(i, i ^ bit) for i in range(size)])  15.8 us
    all_to_all x3, waiting for transfers between devices, exchange(): return lax.all_to_all(parts, axis, 0, 0, tiled=True)  8.01 us
    pallas_call x2, Pallas kernels, spmm_call(): pl.pallas_call(functools.partial(kernel, len(parts)), out_shape=[jax.Shap...  7.34 us
    unnamed x26, local copies, waits for them, and re-layouts  5.1 us
  transfers between devices with their start and end apart: 10, of which 6 were waited for; matrix products, arithmetic and copies ran while one was open for 0% of the time, Pallas kernels for 8%

profile of v2, /device:TPU:16, one launch (start us, length us, event | category | flops | bytes accessed | tf_op | source)
XLA Modules:
  0.0 118.5 jit_solution(14547518342627989584)
XLA Ops:
  0.0 0.8 copy-done.5
  0.9 1.0 copy-done.4
  1.9 13.1 %all-to-all-start = ((bf16[16,128,256]{2,1,0:T(8,128)(2,1)}), bf16[16,128,256]{2,1,0:T(8,128)(2,1)}, u32[]{:S(2)}, u32[]{:S(2)}) async-start(bf16[16,128,256]{2,1,0:T(8,128)(2,1)} %copy-done.4), calls=%async_computation | async-start | bytes 2097152 | tf_op jit(solution)/shard_map/all_to_all | solution.py:211
  15.0 28.5 %all-gather = bf16[1024,256]{1,0:T(8,128)(2,1)} all-gather(bf16[128,256]{1,0:T(8,128)(2,1)S(1)} %copy-done.6), channel_id=2, replica_groups=mesh['zh'=4,'x'=4,'core'=2,'y'=8,'zl'=2] {'y'}, dimensions={0}, use_global_device_ids=true | all-gather | bytes 589824 | tf_op jit(solution)/shard_map/all_gather | solution.py:227
  43.5 1.9 %collective-permute-start.1 = (bf16[16,128,256]{2,1,0:T(8,128)(2,1)}, bf16[16,128,256]{2,1,0:T(8,128)(2,1)}, u32[]{:S(2)}, u32[]{:S(2)}) collective-permute-start(bf16[16,128,256]{2,1,0:T(8,128)(2,1)} %shard_map.92.refs_0_), channel_id=1, source_target_pairs={{0,16},{16,0},{1,17},{17,1},{2,18},{18,2},{3,19},{19,3},{4,20},{20... | collective-permute-start | bytes 3145736 | tf_op jit(solution)/shard_map/ppermute | solution.py:216
  45.4 5.6 %collective-permute-start = (bf16[8,128,256]{2,1,0:T(8,128)(2,1)}, bf16[8,128,256]{2,1,0:T(8,128)(2,1)}, u32[]{:S(2)}, u32[]{:S(2)}) collective-permute-start(bf16[8,128,256]{2,1,0:T(8,128)(2,1)} %bitcast.14), channel_id=1, source_target_pairs={{0,1},{1,0},{2,3},{3,2},{4,5},{5,4},{6,7},{7,6},{8,9},{9,8},{10,11... | collective-permute-start | bytes 1572872 | tf_op jit(solution)/shard_map/ppermute | solution.py:216
  51.8 3.7 %shard_map.93.refs_2_ = bf16[16,128,256]{2,1,0:T(8,128)(2,1)S(1)} custom-call(s32[4]{0:T(128)S(1)} %pad_add_fusion.scalars, s32[96]{0:T(128)S(1)} %bitcast.17, s32[96]{0:T(128)S(1)} %bitcast.19, bf16[96,128,128]{2,1,0:T(8,128)(2,1)S(1)} %bitcast.11, bf16[16,128,256]{2,1,0:T(8,128)(2,1)} %shard_map.92.refs_0_, ...), custom_call_target="tpu_custom_call" | custom-call | flops 805306368 | bytes 8388608 | tf_op jit(solution)/shard_map/pallas_call | solution.py:177
  55.5 0.9 copy-done.1
  56.4 6.9 %all-to-all-start.2 = ((bf16[16,128,256]{2,1,0:T(8,128)(2,1)}), bf16[16,128,256]{2,1,0:T(8,128)(2,1)}, u32[]{:S(2)}, u32[]{:S(2)}) async-start(bf16[16,128,256]{2,1,0:T(8,128)(2,1)} %copy-done.1), calls=%async_computation.2 | async-start | bytes 2097152 | tf_op jit(solution)/shard_map/all_to_all | solution.py:211
  63.9 1.2 %copy-done.2 = bf16[16,128,256]{2,1,0:T(8,128)(2,1)S(1)} copy-done((bf16[16,128,256]{2,1,0:T(8,128)(2,1)S(1)}, bf16[16,128,256]{2,1,0:T(8,128)(2,1)}, u32[]{:S(2)}) %copy-start.2) | copy-done | bytes 1048600
  65.1 1.0 copy-done.3
  66.2 3.6 %shard_map.94 = (bf16[16,128,256]{2,1,0:T(8,128)(2,1)S(1)}, bf16[16,128,256]{2,1,0:T(8,128)(2,1)S(1)}) custom-call(s32[4]{0:T(128)S(1)} %pad_add_fusion.scalars, s32[96]{0:T(128)S(1)} %bitcast.18, s32[96]{0:T(128)S(1)} %bitcast.20, bf16[96,128,128]{2,1,0:T(8,128)(2,1)S(1)} %bitcast.12, bf16[8,128,256]{2,1,0:T(8,128)(2,1)S(1)} %bitcast.15, ...), custom_call_target="tpu_custom_call" | custom-call | flops 805306368 | bytes 8388608 | tf_op jit(solution)/shard_map/pallas_call | solution.py:177
  69.8 2.1 %collective-permute-start.2 = (bf16[16,128,256]{2,1,0:T(8,128)(2,1)S(1)}, bf16[16,128,256]{2,1,0:T(8,128)(2,1)S(1)}, u32[]{:S(2)}, u32[]{:S(2)}) collective-permute-start(bf16[16,128,256]{2,1,0:T(8,128)(2,1)S(1)} %get-tuple-element.14), channel_id=1, source_target_pairs={{0,16},{16,0},{1,17},{17,1},{2,18},{18,2},{3,19},{19,3},{4,20},{20... | collective-permute-start | bytes 3145736 | tf_op jit(solution)/shard_map/ppermute | solution.py:216
  71.9 2.6 %collective-permute-done.2.refs_1_ = bf16[16,128,256]{2,1,0:T(8,128)(2,1)S(1)} collective-permute-done((bf16[16,128,256]{2,1,0:T(8,128)(2,1)S(1)}, bf16[16,128,256]{2,1,0:T(8,128)(2,1)S(1)}, u32[]{:S(2)}, u32[]{:S(2)}) %collective-permute-start.2) | collective-permute-done | bytes 1048608 | tf_op jit(solution)/shard_map/ppermute | solution.py:216
  74.8 5.5 %collective-permute-start.3 = (bf16[4,128,256]{2,1,0:T(8,128)(2,1)S(1)}, bf16[4,128,256]{2,1,0:T(8,128)(2,1)S(1)}, u32[]{:S(2)}, u32[]{:S(2)}) collective-permute-start(bf16[4,128,256]{2,1,0:T(8,128)(2,1)S(1)} %get-tuple-element.16), channel_id=1, source_target_pairs={{0,32},{32,0},{64,96},{96,64},{1,33},{33,1},{65,97},{97,65},{2,34}... | collective-permute-start | bytes 786440 | tf_op jit(solution)/shard_map/ppermute | solution.py:216
  80.3 3.5 %collective-permute-start.4 = (bf16[4,128,256]{2,1,0:T(8,128)(2,1)S(1)}, bf16[4,128,256]{2,1,0:T(8,128)(2,1)S(1)}, u32[]{:S(2)}, u32[]{:S(2)}) collective-permute-start(bf16[4,128,256]{2,1,0:T(8,128)(2,1)S(1)} %get-tuple-element.17), channel_id=1, source_target_pairs={{0,64},{32,96},{64,0},{96,32},{1,65},{33,97},{65,1},{97,33},{2,66}... | collective-permute-start | bytes 786440 | tf_op jit(solution)/shard_map/ppermute | solution.py:216
  83.8 3.0 %collective-permute-start.5 = (bf16[4,128,256]{2,1,0:T(8,128)(2,1)S(1)}, bf16[4,128,256]{2,1,0:T(8,128)(2,1)S(1)}, u32[]{:S(2)}, u32[]{:S(2)}) collective-permute-start(bf16[4,128,256]{2,1,0:T(8,128)(2,1)S(1)} %get-tuple-element.18), channel_id=1, source_target_pairs={{0,96},{32,64},{64,32},{96,0},{1,97},{33,65},{65,33},{97,1},{2,98}... | collective-permute-start | bytes 786440 | tf_op jit(solution)/shard_map/ppermute | solution.py:216
  87.4 6.6 %collective-permute-done.4.refs_2_ = bf16[4,128,256]{2,1,0:T(8,128)(2,1)S(1)} collective-permute-done((bf16[4,128,256]{2,1,0:T(8,128)(2,1)S(1)}, bf16[4,128,256]{2,1,0:T(8,128)(2,1)S(1)}, u32[]{:S(2)}, u32[]{:S(2)}) %collective-permute-start.4) | collective-permute-done | bytes 262176 | tf_op jit(solution)/shard_map/ppermute | solution.py:216
  93.9 5.5 %collective-permute-done.5.refs_3_ = bf16[4,128,256]{2,1,0:T(8,128)(2,1)S(1)} collective-permute-done((bf16[4,128,256]{2,1,0:T(8,128)(2,1)S(1)}, bf16[4,128,256]{2,1,0:T(8,128)(2,1)S(1)}, u32[]{:S(2)}, u32[]{:S(2)}) %collective-permute-start.5) | collective-permute-done | bytes 262176 | tf_op jit(solution)/shard_map/ppermute | solution.py:216
  100.3 6.0 %all-to-all-start.1 = ((bf16[4,128,256]{2,1,0:T(8,128)(2,1)}), bf16[4,128,256]{2,1,0:T(8,128)(2,1)S(1)}, u32[]{:S(2)}, u32[]{:S(2)}) async-start(bf16[4,128,256]{2,1,0:T(8,128)(2,1)} %shard_map.96), calls=%async_computation.1 | async-start | bytes 524288 | tf_op jit(solution)/shard_map/all_to_all | solution.py:211
  106.3 1.4 %shard_map.97 = (bf16[1,128,256]{2,1,0:T(8,128)(2,1)S(1)}, bf16[1,128,256]{2,1,0:T(8,128)(2,1)S(1)}) custom-call(bf16[16,128,256]{2,1,0:T(8,128)(2,1)} %all-to-all-done.2.parts), custom_call_target="tpu_custom_call" | custom-call | flops 524288 | bytes 1572864 | tf_op jit(solution)/shard_map/pallas_call | solution.py:163
  107.7 1.9 %collective-permute-start.6 = (bf16[1,128,256]{2,1,0:T(8,128)(2,1)S(1)}, bf16[1,128,256]{2,1,0:T(8,128)(2,1)S(1)}, u32[]{:S(2)}, u32[]{:S(2)}) collective-permute-start(bf16[1,128,256]{2,1,0:T(8,128)(2,1)S(1)} %get-tuple-element.20), channel_id=1, source_target_pairs={{0,1},{1,0},{2,3},{3,2},{4,5},{5,4},{6,7},{7,6},{8,9},{9,8},{10,11... | collective-permute-start | bytes 196616 | tf_op jit(solution)/shard_map/ppermute | solution.py:216
  109.6 8.0 %all-to-all-done.1.terms_out = bf16[4,128,256]{2,1,0:T(8,128)(2,1)S(1)} async-done(((bf16[4,128,256]{2,1,0:T(8,128)(2,1)}), bf16[4,128,256]{2,1,0:T(8,128)(2,1)S(1)}, u32[]{:S(2)}, u32[]{:S(2)}) %all-to-all-start.1) | async-done | bytes 262176 | tf_op jit(solution)/shard_map/all_to_all | solution.py:211
  117.7 0.9 shard_map.98
  (32 shorter events, 2.4 us)
Async XLA Ops:
  0.0 0.8 copy-start.5
  0.8 14.2 %copy-start.6 = (bf16[128,256]{1,0:T(8,128)(2,1)S(1)}, bf16[128,256]{1,0:T(8,128)(2,1)}, u32[]{:S(2)}) copy-start(bf16[128,256]{1,0:T(8,128)(2,1)} %feats.1) | copy-start | bytes 196612
  0.8 50.9 %copy-start = (bf16[1,1,96,128,128]{4,3,2,1,0:T(8,128)(2,1)S(1)}, bf16[1,1,96,128,128]{4,3,2,1,0:T(8,128)(2,1)}, u32[]{:S(2)}) copy-start(bf16[1,1,96,128,128]{4,3,2,1,0:T(8,128)(2,1)} %param.10) | copy-start | bytes 9437188
  0.8 50.9 %copy-start.10 = (s32[1,1,96]{2,1,0:T(1,128)S(1)}, s32[1,1,96]{2,1,0:T(1,128)}, u32[]{:S(2)}) copy-start(s32[1,1,96]{2,1,0:T(1,128)} %param.11) | copy-start | bytes 1156
  0.8 50.9 %copy-start.11 = (s32[1,1,96]{2,1,0:T(1,128)S(1)}, s32[1,1,96]{2,1,0:T(1,128)}, u32[]{:S(2)}) copy-start(s32[1,1,96]{2,1,0:T(1,128)} %param.12) | copy-start | bytes 1156
  0.9 1.0 copy-start.4
  1.9 41.6 %all-to-all-start = ((bf16[16,128,256]{2,1,0:T(8,128)(2,1)}), bf16[16,128,256]{2,1,0:T(8,128)(2,1)}, u32[]{:S(2)}, u32[]{:S(2)}) async-start(bf16[16,128,256]{2,1,0:T(8,128)(2,1)} %copy-done.4), calls=%async_computation | async-start | bytes 2097152 | tf_op jit(solution)/shard_map/all_to_all | solution.py:211
  43.5 8.2 %collective-permute-start.1 = (bf16[16,128,256]{2,1,0:T(8,128)(2,1)}, bf16[16,128,256]{2,1,0:T(8,128)(2,1)}, u32[]{:S(2)}, u32[]{:S(2)}) collective-permute-start(bf16[16,128,256]{2,1,0:T(8,128)(2,1)} %shard_map.92.refs_0_), channel_id=1, source_target_pairs={{0,16},{16,0},{1,17},{17,1},{2,18},{18,2},{3,19},{19,3},{4,20},{20... | collective-permute-start | bytes 3145736 | tf_op jit(solution)/shard_map/ppermute | solution.py:216
  45.4 18.5 %collective-permute-start = (bf16[8,128,256]{2,1,0:T(8,128)(2,1)}, bf16[8,128,256]{2,1,0:T(8,128)(2,1)}, u32[]{:S(2)}, u32[]{:S(2)}) collective-permute-start(bf16[8,128,256]{2,1,0:T(8,128)(2,1)} %bitcast.14), channel_id=1, source_target_pairs={{0,1},{1,0},{2,3},{3,2},{4,5},{5,4},{6,7},{7,6},{8,9},{9,8},{10,11... | collective-permute-start | bytes 1572872 | tf_op jit(solution)/shard_map/ppermute | solution.py:216
  55.5 1.0 copy-start.1
  56.4 43.8 %all-to-all-start.2 = ((bf16[16,128,256]{2,1,0:T(8,128)(2,1)}), bf16[16,128,256]{2,1,0:T(8,128)(2,1)}, u32[]{:S(2)}, u32[]{:S(2)}) async-start(bf16[16,128,256]{2,1,0:T(8,128)(2,1)} %copy-done.1), calls=%async_computation.2 | async-start | bytes 2097152 | tf_op jit(solution)/shard_map/all_to_all | solution.py:211
  63.9 1.2 %copy-start.2 = (bf16[16,128,256]{2,1,0:T(8,128)(2,1)S(1)}, bf16[16,128,256]{2,1,0:T(8,128)(2,1)}, u32[]{:S(2)}) copy-start(bf16[16,128,256]{2,1,0:T(8,128)(2,1)} %copy-done.1) | copy-start | bytes 3145732
  65.1 1.0 copy-start.3
  69.8 47.9 %copy-start.7 = (bf16[256,256]{1,0:T(8,128)(2,1)S(1)}, bf16[256,256]{1,0:T(8,128)(2,1)}, u32[]{:S(2)}) copy-start(bf16[256,256]{1,0:T(8,128)(2,1)} %w_self.1) | copy-start | bytes 393220
  69.8 47.8 %copy-start.8 = (bf16[256,256]{1,0:T(8,128)(2,1)S(1)}, bf16[256,256]{1,0:T(8,128)(2,1)}, u32[]{:S(2)}) copy-start(bf16[256,256]{1,0:T(8,128)(2,1)} %w_in.1) | copy-start | bytes 393220
  69.8 47.8 %copy-start.9 = (bf16[256,256]{1,0:T(8,128)(2,1)S(1)}, bf16[256,256]{1,0:T(8,128)(2,1)}, u32[]{:S(2)}) copy-start(bf16[256,256]{1,0:T(8,128)(2,1)} %w_out.1) | copy-start | bytes 393220
  69.8 47.8 %copy-start.12 = (f32[256]{0:T(256)S(1)}, f32[256]{0:T(256)}, u32[]{:S(2)}) copy-start(f32[256]{0:T(256)} %param.17) | copy-start | bytes 3076
  69.8 4.7 %collective-permute-start.2 = (bf16[16,128,256]{2,1,0:T(8,128)(2,1)S(1)}, bf16[16,128,256]{2,1,0:T(8,128)(2,1)S(1)}, u32[]{:S(2)}, u32[]{:S(2)}) collective-permute-start(bf16[16,128,256]{2,1,0:T(8,128)(2,1)S(1)} %get-tuple-element.14), channel_id=1, source_target_pairs={{0,16},{16,0},{1,17},{17,1},{2,18},{18,2},{3,19},{19,3},{4,20},{20... | collective-permute-start | bytes 3145736 | tf_op jit(solution)/shard_map/ppermute | solution.py:216
  74.8 12.6 %collective-permute-start.3 = (bf16[4,128,256]{2,1,0:T(8,128)(2,1)S(1)}, bf16[4,128,256]{2,1,0:T(8,128)(2,1)S(1)}, u32[]{:S(2)}, u32[]{:S(2)}) collective-permute-start(bf16[4,128,256]{2,1,0:T(8,128)(2,1)S(1)} %get-tuple-element.16), channel_id=1, source_target_pairs={{0,32},{32,0},{64,96},{96,64},{1,33},{33,1},{65,97},{97,65},{2,34}... | collective-permute-start | bytes 786440 | tf_op jit(solution)/shard_map/ppermute | solution.py:216
  80.3 13.7 %collective-permute-start.4 = (bf16[4,128,256]{2,1,0:T(8,128)(2,1)S(1)}, bf16[4,128,256]{2,1,0:T(8,128)(2,1)S(1)}, u32[]{:S(2)}, u32[]{:S(2)}) collective-permute-start(bf16[4,128,256]{2,1,0:T(8,128)(2,1)S(1)} %get-tuple-element.17), channel_id=1, source_target_pairs={{0,64},{32,96},{64,0},{96,32},{1,65},{33,97},{65,1},{97,33},{2,66}... | collective-permute-start | bytes 786440 | tf_op jit(solution)/shard_map/ppermute | solution.py:216
  83.8 15.6 %collective-permute-start.5 = (bf16[4,128,256]{2,1,0:T(8,128)(2,1)S(1)}, bf16[4,128,256]{2,1,0:T(8,128)(2,1)S(1)}, u32[]{:S(2)}, u32[]{:S(2)}) collective-permute-start(bf16[4,128,256]{2,1,0:T(8,128)(2,1)S(1)} %get-tuple-element.18), channel_id=1, source_target_pairs={{0,96},{32,64},{64,32},{96,0},{1,97},{33,65},{65,33},{97,1},{2,98}... | collective-permute-start | bytes 786440 | tf_op jit(solution)/shard_map/ppermute | solution.py:216
  100.3 17.3 %all-to-all-start.1 = ((bf16[4,128,256]{2,1,0:T(8,128)(2,1)}), bf16[4,128,256]{2,1,0:T(8,128)(2,1)S(1)}, u32[]{:S(2)}, u32[]{:S(2)}) async-start(bf16[4,128,256]{2,1,0:T(8,128)(2,1)} %shard_map.96), calls=%async_computation.1 | async-start | bytes 524288 | tf_op jit(solution)/shard_map/all_to_all | solution.py:211
  107.7 9.9 %collective-permute-start.6 = (bf16[1,128,256]{2,1,0:T(8,128)(2,1)S(1)}, bf16[1,128,256]{2,1,0:T(8,128)(2,1)S(1)}, u32[]{:S(2)}, u32[]{:S(2)}) collective-permute-start(bf16[1,128,256]{2,1,0:T(8,128)(2,1)S(1)} %get-tuple-element.20), channel_id=1, source_target_pairs={{0,1},{1,0},{2,3},{3,2},{4,5},{5,4},{6,7},{7,6},{8,9},{9,8},{10,11... | collective-permute-start | bytes 196616 | tf_op jit(solution)/shard_map/ppermute | solution.py:216

commit v3 on v2

v3 whole, which is shorter than its diff:
```python
import functools

import jax
import jax.numpy as jnp
from jax import lax
from jax.experimental import pallas as pl
from jax.experimental.pallas import tpu as pltpu
from jax.sharding import Mesh, PartitionSpec as P

ZH, X, CORE, YQ, YP, ZL = "zh", "x", "core", "yq", "yp", "zl"
UNROLL = 8
COST = 40000
VMEM_LIMIT = 20 * 2**20
SMEM = pl.BlockSpec(memory_space=pltpu.SMEM)
VMEM = pl.BlockSpec(memory_space=pltpu.VMEM)
ANY = pl.BlockSpec(memory_space=pl.ANY)


def panel_place(block, own):
    return (((block ^ own) & 2) << 2) | ((block >> 2) << 1) | (block & 1)


def col_place(block, own):
    d = block ^ own
    return ((d & 2) << 2) | ((d >> 2) << 1) | (d & 1)


def row_place(block, core):
    return (((block & 1) ^ core) << 4) | (block >> 1)


def walk_slots(count, tiles, product, acc):
    acc[...] = jnp.zeros_like(acc)

    def body(group, _):
        done = []
        for step in range(UNROLL):
            slot = group * UNROLL + step
            tile = jnp.where(slot < count, tiles[slot], jnp.zeros((), tiles.dtype))
            done.append(product(slot, tile))
        for place, value in done:
            acc[place] += value
        return 0

    lax.fori_loop(0, lax.div(count + (UNROLL - 1), UNROLL), body, 0)


def fill(panel, parts):
    start = 0
    for part in parts:
        panel[start : start + part.shape[0]] = part[...]
        start += part.shape[0]


def outward_kernel(parts, scalars, rows, cols, tiles, *refs):
    keep, send, token, panel, acc = refs[-5:]
    fill(panel, refs[:parts])
    core, own = scalars[1], scalars[2]

    def product(slot, tile):
        value = lax.dot_general(
            tile,
            panel[panel_place(rows[slot], own)],
            (((0,), (0,)), ((), ())),
            preferred_element_type=jnp.float32,
        )
        return row_place(cols[slot], core), value

    walk_slots(scalars[0], tiles, product, acc)
    keep[...] = acc[:16].astype(keep.dtype)
    send[...] = acc[16:].astype(send.dtype)
    token[...] = jnp.zeros_like(token)


def inward_kernel(parts, scalars, rows, cols, tiles, *refs):
    keep, send, token, panel, acc = refs[-5:]
    fill(panel, refs[:parts])
    core, own = scalars[1], scalars[2]

    def product(slot, tile):
        value = jnp.dot(
            tile, panel[row_place(cols[slot], core)], preferred_element_type=jnp.float32
        )
        return col_place(rows[slot], own), value

    walk_slots(scalars[0], tiles, product, acc)
    keep[...] = acc[:8].astype(keep.dtype)
    send[...] = acc[8:].astype(send.dtype)
    token[...] = jnp.zeros_like(token)


def add_kernel(terms, pieces, *refs):
    outs = refs[len(refs) - pieces :]
    size = outs[0].shape[0]
    for k, out in enumerate(outs):
        part = pl.ds(k * size, size)
        total = refs[0][part].astype(jnp.float32)
        for ref in refs[1:terms]:
            total = total + ref[part].astype(jnp.float32)
        out[...] = total.astype(out.dtype)


def final_kernel(feats, w_self, w_in, w_out, bias, terms_out, *refs):
    *terms_in, out = refs

    def product(terms, weight):
        total = terms[0].astype(jnp.float32)
        for term in terms[1:]:
            total = total + term.astype(jnp.float32)
        return jnp.dot(
            total.astype(jnp.bfloat16), weight[...], preferred_element_type=jnp.float32
        )

    total = jnp.dot(feats[...], w_self[...], preferred_element_type=jnp.float32)
    total = total + product([term[0] for term in terms_in], w_in)
    total = total + product([terms_out[k] for k in range(terms_out.shape[0])], w_out)
    out[...] = jnp.maximum(total + bias[...], 0.0).astype(out.dtype)


def copies_kernel(value, *refs):
    out = refs[-1]
    size = value.shape[0]
    for k in range(out.shape[0] // size):
        out[k * size : (k + 1) * size] = value[...]


def copies_call(value, count, after):
    return pl.pallas_call(
        copies_kernel,
        out_shape=jax.ShapeDtypeStruct((count * value.shape[0], *value.shape[1:]), value.dtype),
        in_specs=[VMEM, ANY],
        out_specs=VMEM,
        compiler_params=pltpu.CompilerParams(vmem_limit_bytes=VMEM_LIMIT),
        cost_estimate=pl.CostEstimate(
            flops=0, bytes_accessed=2 * (count + 1) * value.size, transcendentals=0
        ),
    )(value, after)


def spmm_call(kernel, out_tiles, panel_tiles, scalars, rows, cols, tiles, parts, after=()):
    side, width = tiles.shape[-1], parts[0].shape[-1]
    half = jax.ShapeDtypeStruct((out_tiles // 2, side, width), jnp.bfloat16)
    return pl.pallas_call(
        functools.partial(kernel, len(parts)),
        out_shape=[half, half, jax.ShapeDtypeStruct((8, 128), jnp.float32)],
        in_specs=[SMEM] * 3 + [VMEM] * (1 + len(parts) + len(after)),
        out_specs=[VMEM] * 3,
        scratch_shapes=[
            pltpu.VMEM((panel_tiles, side, width), jnp.bfloat16),
            pltpu.VMEM((out_tiles, side, width), jnp.float32),
        ],
        compiler_params=pltpu.CompilerParams(vmem_limit_bytes=VMEM_LIMIT),
        cost_estimate=pl.CostEstimate(
            flops=2 * tiles.shape[0] * side * side * width,
            bytes_accessed=8 * 2**20,
            transcendentals=0,
        ),
    )(scalars, rows, cols, tiles, *parts, *after)


def add_call(terms, pieces, after=(), cost=1):
    count, side, width = terms[0].shape
    size = terms[0].size
    return pl.pallas_call(
        functools.partial(add_kernel, len(terms), pieces),
        out_shape=[jax.ShapeDtypeStruct((count // pieces, side, width), jnp.bfloat16)] * pieces,
        in_specs=[VMEM] * (len(terms) + len(after)),
        out_specs=[VMEM] * pieces,
        compiler_params=pltpu.CompilerParams(vmem_limit_bytes=VMEM_LIMIT),
        cost_estimate=pl.CostEstimate(
            flops=cost * size * len(terms),
            bytes_accessed=2 * size * (len(terms) + 1),
            transcendentals=0,
        ),
    )(*terms, *after)


def exchange(parts, axis):
    return lax.all_to_all(parts, axis, 0, 0, tiled=True)


def swap(value, axis, bit):
    size = lax.axis_size(axis)
    return lax.ppermute(value, axis, [(i, i ^ bit) for i in range(size)])


def per_device(feats, tiles, tile_rows, tile_cols, tile_count, w_self, w_in, w_out, bias):
    tiles, rows, cols = tiles[0, 0], tile_rows[0, 0], tile_cols[0, 0]
    side, width = feats.shape
    own_col = lax.axis_index(YQ) * 4 + lax.axis_index(YP) * 2 + lax.axis_index(ZL)
    scalars = jnp.stack([tile_count[0, 0], lax.axis_index(CORE), own_col]).astype(jnp.int32)

    near_row = lax.all_gather(feats, ZL)
    near_col = exchange(copies_call(feats[None], 16, near_row), (ZH, X))
    far_col = swap(near_col, CORE, 1)
    near_row = lax.all_gather(near_row, YQ, axis=0, tiled=True)
    far_row = swap(near_row, YP, 1)

    keep_out, send_out, token = spmm_call(
        outward_kernel, 32, 16, scalars, rows, cols, tiles, (near_row, far_row)
    )
    got_out = swap(send_out, CORE, 1)
    keep, send, token = spmm_call(
        inward_kernel, 16, 32, scalars, rows, cols, tiles, (near_col, far_col), (token,)
    )
    (both,) = add_call([keep_out, got_out], 1, after=(token,))
    terms_out = exchange(both, (ZH, X))
    parts = add_call([keep, swap(send, YP, 1)], 4, cost=COST)
    got = [swap(part, YQ, bit) for part, bit in zip(parts[1:], (1, 2, 3))]
    keep, send = add_call([parts[0], *got], 2)
    terms_in = [keep, swap(send, ZL, 1)]
    return pl.pallas_call(
        final_kernel,
        out_shape=jax.ShapeDtypeStruct((side, width), jnp.bfloat16),
        in_specs=[VMEM] * 8,
        out_specs=VMEM,
        compiler_params=pltpu.CompilerParams(vmem_limit_bytes=VMEM_LIMIT),
    )(feats, w_self, w_in, w_out, bias[None, :], terms_out, *terms_in)


def solution(mesh):
    split = Mesh(mesh.devices.reshape(4, 4, 2, 4, 2, 2), (ZH, X, CORE, YQ, YP, ZL))
    row, col = (ZH, X, CORE), (YQ, YP, ZL)
    in_specs = (
        P(row + col, None),
        P(row, col, None, None, None),
        P(row, col, None),
        P(row, col, None),
        P(row, col),
        P(),
        P(),
        P(),
        P(),
    )
    return jax.shard_map(
        per_device, mesh=split, in_specs=in_specs, out_specs=P(row + col, None), check_vma=False
    )
```

time: 119 us -> 113 us (0.950)
  the two profiles are of different devices: /device:TPU:16 before, /device:TPU:10 now
where the time goes in v3:
time: 113 us; the launch traced here: 112 us
  starting transfers between devices  53.3 us (47%)
  blocking collectives  23.8 us (21%)
  waiting for transfers between devices  17.3 us (15%)
  Pallas kernels  14.6 us (13%)
  local copies, waits for them, and re-layouts  2.63 us (2%)
    ppermute x8, starting transfers between devices, swap(): return lax.ppermute(value, axis, [(i, i ^ bit) for i in range(size)])  29.1 us
    all_to_all x2, starting transfers between devices, exchange(): return lax.all_to_all(parts, axis, 0, 0, tiled=True)  24.2 us
    all_gather x1, blocking collectives, per_device(): near_row = lax.all_gather(near_row, YQ, axis=0, tiled=True)  18.1 us
    ppermute x8, waiting for transfers between devices, swap(): return lax.ppermute(value, axis, [(i, i ^ bit) for i in range(size)])  17.3 us
    pallas_call x2, Pallas kernels, spmm_call(): pl.pallas_call(functools.partial(kernel, len(parts)), out_shape=[half, ha...  12.1 us
    all_gather x1, blocking collectives, per_device(): near_row = lax.all_gather(feats, ZL)  5.63 us
    unnamed x24, local copies, waits for them, and re-layouts  2.63 us
  transfers between devices with their start and end apart: 10, of which 4 were waited for; matrix products, arithmetic and copies ran while one was open for 0% of the time, Pallas kernels for 12%

profile of v3, /device:TPU:10, one launch (start us, length us, event | category | flops | bytes accessed | tf_op | source)
XLA Modules:
  0.0 112.5 jit_solution(3420516467326424799)
XLA Ops:
  0.0 5.6 %all-gather = bf16[256,256]{1,0:T(8,128)(2,1)S(1)} all-gather(bf16[128,256]{1,0:T(8,128)(2,1)} %feats.1), channel_id=2, replica_groups=mesh['zh'=4,'x'=4,'core'=2,'yq'=4,'yp'=2,'zl'=2] {'zl'}, dimensions={0}, use_global_device_ids=true | all-gather | bytes 196608 | tf_op jit(solution)/shard_map/all_gather | solution.py:193
  5.6 0.8 copy-done.2
  6.6 0.9 copy-done.1
  7.5 13.0 %all-to-all-start = ((bf16[16,128,256]{2,1,0:T(8,128)(2,1)}), bf16[16,128,256]{2,1,0:T(8,128)(2,1)}, u32[]{:S(2)}, u32[]{:S(2)}) async-start(bf16[16,128,256]{2,1,0:T(8,128)(2,1)} %copy-done.1), calls=%async_computation | async-start | bytes 2097152 | tf_op jit(solution)/shard_map/all_to_all | solution.py:179
  20.5 18.1 %all_gather.11.refs_0_ = bf16[8,128,256]{2,1,0:T(8,128)(2,1)} all-gather(bf16[2,128,256]{2,1,0:T(8,128)(2,1)S(1)} %bitcast.13), channel_id=1, replica_groups=mesh['zh'=4,'x'=4,'core'=2,'yq'=4,'yp'=2,'zl'=2] {'yq'}, dimensions={0}, use_global_device_ids=true | all-gather | bytes 655360 | tf_op jit(solution)/shard_map/all_gather | solution.py:196
  38.6 4.2 %collective-permute-start = (bf16[8,128,256]{2,1,0:T(8,128)(2,1)}, bf16[8,128,256]{2,1,0:T(8,128)(2,1)}, u32[]{:S(2)}, u32[]{:S(2)}) collective-permute-start(bf16[8,128,256]{2,1,0:T(8,128)(2,1)} %all_gather.11.refs_0_), channel_id=1, source_target_pairs={{0,2},{2,0},{1,3},{3,1},{4,6},{6,4},{5,7},{7,5},{8,10},{10,8},{9,1... | collective-permute-start | bytes 1572872 | tf_op jit(solution)/shard_map/ppermute | solution.py:184
  42.8 1.9 %collective-permute-start.2 = (bf16[16,128,256]{2,1,0:T(8,128)(2,1)}, bf16[16,128,256]{2,1,0:T(8,128)(2,1)}, u32[]{:S(2)}, u32[]{:S(2)}) collective-permute-start(bf16[16,128,256]{2,1,0:T(8,128)(2,1)} %all-to-all-done.refs_0_), channel_id=1, source_target_pairs={{0,16},{16,0},{1,17},{17,1},{2,18},{18,2},{3,19},{19,3},{4,20},{20... | collective-permute-start | bytes 3145736 | tf_op jit(solution)/shard_map/ppermute | solution.py:184
  45.5 5.5 %collective-permute-done.refs_1_ = bf16[8,128,256]{2,1,0:T(8,128)(2,1)} collective-permute-done((bf16[8,128,256]{2,1,0:T(8,128)(2,1)}, bf16[8,128,256]{2,1,0:T(8,128)(2,1)}, u32[]{:S(2)}, u32[]{:S(2)}) %collective-permute-start) | collective-permute-done | bytes 524320 | tf_op jit(solution)/shard_map/ppermute | solution.py:184
  51.0 5.8 %shard_map.91 = (bf16[16,128,256]{2,1,0:T(8,128)(2,1)S(1)}, bf16[16,128,256]{2,1,0:T(8,128)(2,1)S(1)}, f32[8,128]{1,0:T(8,128)S(1)}) custom-call(s32[3]{0:T(128)S(1)} %pad_add_fusion.scalars, s32[96]{0:T(128)S(1)} %bitcast.15, s32[96]{0:T(128)S(1)} %bitcast.17, bf16[96,128,128]{2,1,0:T(8,128)(2,1)S(1)} %bitcast.10, bf16[8,128,256]{2,1,0:T(8,128)(2,1)} %all_gather.11.refs_0_, ...), custom_call_target="tpu_custom_call" | custom-call | flops 805306368 | bytes 8388608 | tf_op jit(solution)/shard_map/pallas_call | solution.py:143
  56.8 1.9 %collective-permute-start.1 = (bf16[16,128,256]{2,1,0:T(8,128)(2,1)S(1)}, bf16[16,128,256]{2,1,0:T(8,128)(2,1)S(1)}, u32[]{:S(2)}, u32[]{:S(2)}) collective-permute-start(bf16[16,128,256]{2,1,0:T(8,128)(2,1)S(1)} %get-tuple-element.18), channel_id=1, source_target_pairs={{0,16},{16,0},{1,17},{17,1},{2,18},{18,2},{3,19},{19,3},{4,20},{20... | collective-permute-start | bytes 3145736 | tf_op jit(solution)/shard_map/ppermute | solution.py:184
  58.8 6.3 %shard_map.93 = (bf16[8,128,256]{2,1,0:T(8,128)(2,1)S(1)}, bf16[8,128,256]{2,1,0:T(8,128)(2,1)}, f32[8,128]{1,0:T(8,128)S(1)}) custom-call(s32[3]{0:T(128)S(1)} %pad_add_fusion.scalars, s32[96]{0:T(128)S(1)} %bitcast.16, s32[96]{0:T(128)S(1)} %bitcast.18, bf16[96,128,128]{2,1,0:T(8,128)(2,1)S(1)} %bitcast.11, bf16[16,128,256]{2,1,0:T(8,128)(2,1)} %all-to-all-done.refs_0_, ...), custom_call_target="tpu_custom_call" | custom-call | flops 805306368 | bytes 8388608 | tf_op jit(solution)/shard_map/pallas_call | solution.py:143
  65.1 0.8 copy-done.10
  65.9 2.0 %collective-permute-start.3 = (bf16[8,128,256]{2,1,0:T(8,128)(2,1)}, bf16[8,128,256]{2,1,0:T(8,128)(2,1)S(1)}, u32[]{:S(2)}, u32[]{:S(2)}) collective-permute-start(bf16[8,128,256]{2,1,0:T(8,128)(2,1)} %get-tuple-element.22), channel_id=1, source_target_pairs={{0,2},{2,0},{1,3},{3,1},{4,6},{6,4},{5,7},{7,5},{8,10},{10,8},{9,1... | collective-permute-start | bytes 1572872 | tf_op jit(solution)/shard_map/ppermute | solution.py:184
  67.9 1.3 %shard_map.94 = bf16[16,128,256]{2,1,0:T(8,128)(2,1)} custom-call(bf16[16,128,256]{2,1,0:T(8,128)(2,1)S(1)} %get-tuple-element.17.refs_0_, bf16[16,128,256]{2,1,0:T(8,128)(2,1)S(1)} %collective-permute-done.1.refs_1_, f32[8,128]{1,0:T(8,128)S(1)} %get-tuple-element.20.refs_2_), custom_call_target="tpu_custom_call" | custom-call | flops 1048576 | bytes 3145728 | tf_op jit(solution)/shard_map/pallas_call | solution.py:164
  69.2 11.2 %all-to-all-start.1 = ((bf16[16,128,256]{2,1,0:T(8,128)(2,1)}), bf16[16,128,256]{2,1,0:T(8,128)(2,1)S(1)}, u32[]{:S(2)}, u32[]{:S(2)}) async-start(bf16[16,128,256]{2,1,0:T(8,128)(2,1)} %shard_map.94), calls=%async_computation.1 | async-start | bytes 2097152 | tf_op jit(solution)/shard_map/all_to_all | solution.py:179
  80.5 0.1 shard_map.95
  80.6 2.8 %collective-permute-start.4 = (bf16[2,128,256]{2,1,0:T(8,128)(2,1)S(1)}, bf16[2,128,256]{2,1,0:T(8,128)(2,1)S(1)}, u32[]{:S(2)}, u32[]{:S(2)}) collective-permute-start(bf16[2,128,256]{2,1,0:T(8,128)(2,1)S(1)} %get-tuple-element.24), channel_id=1, source_target_pairs={{0,4},{4,0},{8,12},{12,8},{1,5},{5,1},{9,13},{13,9},{2,6},{6,2},{1... | collective-permute-start | bytes 393224 | tf_op jit(solution)/shard_map/ppermute | solution.py:184
  83.5 2.9 %collective-permute-start.5 = (bf16[2,128,256]{2,1,0:T(8,128)(2,1)S(1)}, bf16[2,128,256]{2,1,0:T(8,128)(2,1)S(1)}, u32[]{:S(2)}, u32[]{:S(2)}) collective-permute-start(bf16[2,128,256]{2,1,0:T(8,128)(2,1)S(1)} %get-tuple-element.25), channel_id=1, source_target_pairs={{0,8},{4,12},{8,0},{12,4},{1,9},{5,13},{9,1},{13,5},{2,10},{6,14},... | collective-permute-start | bytes 393224 | tf_op jit(solution)/shard_map/ppermute | solution.py:184
  86.4 6.6 %collective-permute-start.6 = (bf16[2,128,256]{2,1,0:T(8,128)(2,1)S(1)}, bf16[2,128,256]{2,1,0:T(8,128)(2,1)S(1)}, u32[]{:S(2)}, u32[]{:S(2)}) collective-permute-start(bf16[2,128,256]{2,1,0:T(8,128)(2,1)S(1)} %get-tuple-element.26), channel_id=1, source_target_pairs={{0,12},{4,8},{8,4},{12,0},{1,13},{5,9},{9,5},{13,1},{2,14},{6,10},... | collective-permute-start | bytes 393224 | tf_op jit(solution)/shard_map/ppermute | solution.py:184
  93.0 5.0 %collective-permute-done.5.refs_2_ = bf16[2,128,256]{2,1,0:T(8,128)(2,1)S(1)} collective-permute-done((bf16[2,128,256]{2,1,0:T(8,128)(2,1)S(1)}, bf16[2,128,256]{2,1,0:T(8,128)(2,1)S(1)}, u32[]{:S(2)}, u32[]{:S(2)}) %collective-permute-start.5) | collective-permute-done | bytes 131104 | tf_op jit(solution)/shard_map/ppermute | solution.py:184
  98.0 4.5 %collective-permute-done.6.refs_3_ = bf16[2,128,256]{2,1,0:T(8,128)(2,1)S(1)} collective-permute-done((bf16[2,128,256]{2,1,0:T(8,128)(2,1)S(1)}, bf16[2,128,256]{2,1,0:T(8,128)(2,1)S(1)}, u32[]{:S(2)}, u32[]{:S(2)}) %collective-permute-start.6) | collective-permute-done | bytes 131104 | tf_op jit(solution)/shard_map/ppermute | solution.py:184
  102.6 6.6 %collective-permute-start.7 = (bf16[1,128,256]{2,1,0:T(8,128)(2,1)S(1)}, bf16[1,128,256]{2,1,0:T(8,128)(2,1)S(1)}, u32[]{:S(2)}, u32[]{:S(2)}) collective-permute-start(bf16[1,128,256]{2,1,0:T(8,128)(2,1)S(1)} %get-tuple-element.28), channel_id=1, source_target_pairs={{0,1},{1,0},{2,3},{3,2},{4,5},{5,4},{6,7},{7,6},{8,9},{9,8},{10,11... | collective-permute-start | bytes 196616 | tf_op jit(solution)/shard_map/ppermute | solution.py:184
  109.2 2.2 %collective-permute-done.7.refs_1_ = bf16[1,128,256]{2,1,0:T(8,128)(2,1)S(1)} collective-permute-done((bf16[1,128,256]{2,1,0:T(8,128)(2,1)S(1)}, bf16[1,128,256]{2,1,0:T(8,128)(2,1)S(1)}, u32[]{:S(2)}, u32[]{:S(2)}) %collective-permute-start.7) | collective-permute-done | bytes 65568 | tf_op jit(solution)/shard_map/ppermute | solution.py:184
  111.5 1.0 shard_map.97
  (30 shorter events, 0.3 us)
Async XLA Ops:
  0.0 51.0 %copy-start = (bf16[1,1,96,128,128]{4,3,2,1,0:T(8,128)(2,1)S(1)}, bf16[1,1,96,128,128]{4,3,2,1,0:T(8,128)(2,1)}, u32[]{:S(2)}) copy-start(bf16[1,1,96,128,128]{4,3,2,1,0:T(8,128)(2,1)} %param.10) | copy-start | bytes 9437188
  5.6 0.8 copy-start.2
  6.5 44.6 %copy-start.7 = (s32[1,1,96]{2,1,0:T(1,128)S(1)}, s32[1,1,96]{2,1,0:T(1,128)}, u32[]{:S(2)}) copy-start(s32[1,1,96]{2,1,0:T(1,128)} %param.11) | copy-start | bytes 1156
  6.5 44.6 %copy-start.8 = (s32[1,1,96]{2,1,0:T(1,128)S(1)}, s32[1,1,96]{2,1,0:T(1,128)}, u32[]{:S(2)}) copy-start(s32[1,1,96]{2,1,0:T(1,128)} %param.12) | copy-start | bytes 1156
  6.5 0.9 copy-start.1
  7.5 35.3 %all-to-all-start = ((bf16[16,128,256]{2,1,0:T(8,128)(2,1)}), bf16[16,128,256]{2,1,0:T(8,128)(2,1)}, u32[]{:S(2)}, u32[]{:S(2)}) async-start(bf16[16,128,256]{2,1,0:T(8,128)(2,1)} %copy-done.1), calls=%async_computation | async-start | bytes 2097152 | tf_op jit(solution)/shard_map/all_to_all | solution.py:179
  38.6 12.4 %collective-permute-start = (bf16[8,128,256]{2,1,0:T(8,128)(2,1)}, bf16[8,128,256]{2,1,0:T(8,128)(2,1)}, u32[]{:S(2)}, u32[]{:S(2)}) collective-permute-start(bf16[8,128,256]{2,1,0:T(8,128)(2,1)} %all_gather.11.refs_0_), channel_id=1, source_target_pairs={{0,2},{2,0},{1,3},{3,1},{4,6},{6,4},{5,7},{7,5},{8,10},{10,8},{9,1... | collective-permute-start | bytes 1572872 | tf_op jit(solution)/shard_map/ppermute | solution.py:184
  42.8 16.0 %collective-permute-start.2 = (bf16[16,128,256]{2,1,0:T(8,128)(2,1)}, bf16[16,128,256]{2,1,0:T(8,128)(2,1)}, u32[]{:S(2)}, u32[]{:S(2)}) collective-permute-start(bf16[16,128,256]{2,1,0:T(8,128)(2,1)} %all-to-all-done.refs_0_), channel_id=1, source_target_pairs={{0,16},{16,0},{1,17},{17,1},{2,18},{18,2},{3,19},{19,3},{4,20},{20... | collective-permute-start | bytes 3145736 | tf_op jit(solution)/shard_map/ppermute | solution.py:184
  56.8 11.1 %collective-permute-start.1 = (bf16[16,128,256]{2,1,0:T(8,128)(2,1)S(1)}, bf16[16,128,256]{2,1,0:T(8,128)(2,1)S(1)}, u32[]{:S(2)}, u32[]{:S(2)}) collective-permute-start(bf16[16,128,256]{2,1,0:T(8,128)(2,1)S(1)} %get-tuple-element.18), channel_id=1, source_target_pairs={{0,16},{16,0},{1,17},{17,1},{2,18},{18,2},{3,19},{19,3},{4,20},{20... | collective-permute-start | bytes 3145736 | tf_op jit(solution)/shard_map/ppermute | solution.py:184
  65.1 0.8 copy-start.10
  65.9 14.6 %copy-start.11 = (bf16[8,128,256]{2,1,0:T(8,128)(2,1)S(1)}, bf16[8,128,256]{2,1,0:T(8,128)(2,1)}, u32[]{:S(2)}) copy-start(bf16[8,128,256]{2,1,0:T(8,128)(2,1)} %copy-done.10) | copy-start | bytes 1572868
  65.9 14.6 %collective-permute-start.3 = (bf16[8,128,256]{2,1,0:T(8,128)(2,1)}, bf16[8,128,256]{2,1,0:T(8,128)(2,1)S(1)}, u32[]{:S(2)}, u32[]{:S(2)}) collective-permute-start(bf16[8,128,256]{2,1,0:T(8,128)(2,1)} %get-tuple-element.22), channel_id=1, source_target_pairs={{0,2},{2,0},{1,3},{3,1},{4,6},{6,4},{5,7},{7,5},{8,10},{10,8},{9,1... | collective-permute-start | bytes 1572872 | tf_op jit(solution)/shard_map/ppermute | solution.py:184
  69.2 42.3 %all-to-all-start.1 = ((bf16[16,128,256]{2,1,0:T(8,128)(2,1)}), bf16[16,128,256]{2,1,0:T(8,128)(2,1)S(1)}, u32[]{:S(2)}, u32[]{:S(2)}) async-start(bf16[16,128,256]{2,1,0:T(8,128)(2,1)} %shard_map.94), calls=%async_computation.1 | async-start | bytes 2097152 | tf_op jit(solution)/shard_map/all_to_all | solution.py:179
  80.5 31.0 %copy-start.3 = (bf16[128,256]{1,0:T(8,128)(2,1)S(1)}, bf16[128,256]{1,0:T(8,128)(2,1)}, u32[]{:S(2)}) copy-start(bf16[128,256]{1,0:T(8,128)(2,1)} %feats.1) | copy-start | bytes 196612
  80.5 31.0 %copy-start.4 = (bf16[256,256]{1,0:T(8,128)(2,1)S(1)}, bf16[256,256]{1,0:T(8,128)(2,1)}, u32[]{:S(2)}) copy-start(bf16[256,256]{1,0:T(8,128)(2,1)} %w_self.1) | copy-start | bytes 393220
  80.5 31.0 %copy-start.5 = (bf16[256,256]{1,0:T(8,128)(2,1)S(1)}, bf16[256,256]{1,0:T(8,128)(2,1)}, u32[]{:S(2)}) copy-start(bf16[256,256]{1,0:T(8,128)(2,1)} %w_in.1) | copy-start | bytes 393220
  80.5 31.0 %copy-start.6 = (bf16[256,256]{1,0:T(8,128)(2,1)S(1)}, bf16[256,256]{1,0:T(8,128)(2,1)}, u32[]{:S(2)}) copy-start(bf16[256,256]{1,0:T(8,128)(2,1)} %w_out.1) | copy-start | bytes 393220
  80.5 31.0 %copy-start.9 = (f32[256]{0:T(256)S(1)}, f32[256]{0:T(256)}, u32[]{:S(2)}) copy-start(f32[256]{0:T(256)} %param.17) | copy-start | bytes 3076
  80.6 12.4 %collective-permute-start.4 = (bf16[2,128,256]{2,1,0:T(8,128)(2,1)S(1)}, bf16[2,128,256]{2,1,0:T(8,128)(2,1)S(1)}, u32[]{:S(2)}, u32[]{:S(2)}) collective-permute-start(bf16[2,128,256]{2,1,0:T(8,128)(2,1)S(1)} %get-tuple-element.24), channel_id=1, source_target_pairs={{0,4},{4,0},{8,12},{12,8},{1,5},{5,1},{9,13},{13,9},{2,6},{6,2},{1... | collective-permute-start | bytes 393224 | tf_op jit(solution)/shard_map/ppermute | solution.py:184
  83.5 14.5 %collective-permute-start.5 = (bf16[2,128,256]{2,1,0:T(8,128)(2,1)S(1)}, bf16[2,128,256]{2,1,0:T(8,128)(2,1)S(1)}, u32[]{:S(2)}, u32[]{:S(2)}) collective-permute-start(bf16[2,128,256]{2,1,0:T(8,128)(2,1)S(1)} %get-tuple-element.25), channel_id=1, source_target_pairs={{0,8},{4,12},{8,0},{12,4},{1,9},{5,13},{9,1},{13,5},{2,10},{6,14},... | collective-permute-start | bytes 393224 | tf_op jit(solution)/shard_map/ppermute | solution.py:184
  86.4 16.1 %collective-permute-start.6 = (bf16[2,128,256]{2,1,0:T(8,128)(2,1)S(1)}, bf16[2,128,256]{2,1,0:T(8,128)(2,1)S(1)}, u32[]{:S(2)}, u32[]{:S(2)}) collective-permute-start(bf16[2,128,256]{2,1,0:T(8,128)(2,1)S(1)} %get-tuple-element.26), channel_id=1, source_target_pairs={{0,12},{4,8},{8,4},{12,0},{1,13},{5,9},{9,5},{13,1},{2,14},{6,10},... | collective-permute-start | bytes 393224 | tf_op jit(solution)/shard_map/ppermute | solution.py:184
  102.6 8.9 %collective-permute-start.7 = (bf16[1,128,256]{2,1,0:T(8,128)(2,1)S(1)}, bf16[1,128,256]{2,1,0:T(8,128)(2,1)S(1)}, u32[]{:S(2)}, u32[]{:S(2)}) collective-permute-start(bf16[1,128,256]{2,1,0:T(8,128)(2,1)S(1)} %get-tuple-element.28), channel_id=1, source_target_pairs={{0,1},{1,0},{2,3},{3,2},{4,5},{5,4},{6,7},{7,6},{8,9},{9,8},{10,11... | collective-permute-start | bytes 196616 | tf_op jit(solution)/shard_map/ppermute | solution.py:184

commit v4 on v3

--- a/solution.py
+++ b/solution.py
@@ -8,8 +8,10 @@
 from jax.sharding import Mesh, PartitionSpec as P
 
 ZH, X, CORE, YQ, YP, ZL = "zh", "x", "core", "yq", "yp", "zl"
-UNROLL = 8
-COST = 40000
+UNROLL = 32
+COST = 20000
+COST2 = 40000
+TIE_COST = 10**11
 VMEM_LIMIT = 20 * 2**20
 SMEM = pl.BlockSpec(memory_space=pltpu.SMEM)
 VMEM = pl.BlockSpec(memory_space=pltpu.VMEM)
@@ -27,6 +29,10 @@
 
 def row_place(block, core):
     return (((block & 1) ^ core) << 4) | (block >> 1)
+
+
+def term_place(block):
+    return ((block & 1) << 4) | ((block & 6) << 1) | (block >> 3)
 
 
 def walk_slots(count, tiles, product, acc):
@@ -53,9 +59,9 @@
 
 
 def outward_kernel(parts, scalars, rows, cols, tiles, *refs):
-    keep, send, token, panel, acc = refs[-5:]
+    out, token, panel, acc = refs[-4:]
     fill(panel, refs[:parts])
-    core, own = scalars[1], scalars[2]
+    own = scalars[2]
 
     def product(slot, tile):
         value = lax.dot_general(
@@ -64,11 +70,10 @@
             (((0,), (0,)), ((), ())),
             preferred_element_type=jnp.float32,
         )
-        return row_place(cols[slot], core), value
+        return term_place(cols[slot]), value
 
     walk_slots(scalars[0], tiles, product, acc)
-    keep[...] = acc[:16].astype(keep.dtype)
-    send[...] = acc[16:].astype(send.dtype)
+    out[...] = acc[...].astype(out.dtype)
     token[...] = jnp.zeros_like(token)
 
 
@@ -137,14 +142,52 @@
     )(value, after)
 
 
-def spmm_call(kernel, out_tiles, panel_tiles, scalars, rows, cols, tiles, parts, after=()):
+def tie_kernel(value, *refs):
+    refs[-1][...] = value[...]
+
+
+def tie_call(value, after, cost=0):
+    return pl.pallas_call(
+        tie_kernel,
+        out_shape=jax.ShapeDtypeStruct(value.shape, value.dtype),
+        in_specs=[VMEM] + [ANY] * len(after),
+        out_specs=VMEM,
+        compiler_params=pltpu.CompilerParams(vmem_limit_bytes=VMEM_LIMIT),
+        cost_estimate=pl.CostEstimate(
+            flops=cost, bytes_accessed=4 * value.size, transcendentals=0
+        ),
+    )(value, *after)
+
+
+def fold_kernel(parts, out):
+    size = out.shape[0]
+    total = parts[:size].astype(jnp.float32)
+    for start in range(size, parts.shape[0], size):
+        total = total + parts[start : start + size].astype(jnp.float32)
+    out[...] = total.astype(out.dtype)
+
+
+def fold_call(parts, count):
+    return pl.pallas_call(
+        fold_kernel,
+        out_shape=jax.ShapeDtypeStruct((parts.shape[0] // count, *parts.shape[1:]), parts.dtype),
+        in_specs=[VMEM],
+        out_specs=VMEM,
+        compiler_params=pltpu.CompilerParams(vmem_limit_bytes=VMEM_LIMIT),
+        cost_estimate=pl.CostEstimate(
+            flops=parts.size, bytes_accessed=3 * parts.size, transcendentals=0
+        ),
+    )(parts)
+
+
+def spmm_call(kernel, out_tiles, panel_tiles, scalars, rows, cols, tiles, parts, after=(), outs=2):
     side, width = tiles.shape[-1], parts[0].shape[-1]
-    half = jax.ShapeDtypeStruct((out_tiles // 2, side, width), jnp.bfloat16)
+    part = jax.ShapeDtypeStruct((out_tiles // outs, side, width), jnp.bfloat16)
     return pl.pallas_call(
         functools.partial(kernel, len(parts)),
-        out_shape=[half, half, jax.ShapeDtypeStruct((8, 128), jnp.float32)],
+        out_shape=[part] * outs + [jax.ShapeDtypeStruct((8, 128), jnp.float32)],
         in_specs=[SMEM] * 3 + [VMEM] * (1 + len(parts) + len(after)),
-        out_specs=[VMEM] * 3,
+        out_specs=[VMEM] * (outs + 1),
         scratch_shapes=[
             pltpu.VMEM((panel_tiles, side, width), jnp.bfloat16),
             pltpu.VMEM((out_tiles, side, width), jnp.float32),
@@ -192,22 +235,30 @@
 
     near_row = lax.all_gather(feats, ZL)
     near_col = exchange(copies_call(feats[None], 16, near_row), (ZH, X))
+    near_row = lax.all_gather(near_row, YQ, axis=0, tiled=True)
+    far_row = tie_call(swap(near_row, YP, 1), (), TIE_COST)
+    near_col = tie_call(near_col, (near_row,))
     far_col = swap(near_col, CORE, 1)
-    near_row = lax.all_gather(near_row, YQ, axis=0, tiled=True)
-    far_row = swap(near_row, YP, 1)
-
-    keep_out, send_out, token = spmm_call(
-        outward_kernel, 32, 16, scalars, rows, cols, tiles, (near_row, far_row)
-    )
-    got_out = swap(send_out, CORE, 1)
+
     keep, send, token = spmm_call(
-        inward_kernel, 16, 32, scalars, rows, cols, tiles, (near_col, far_col), (token,)
-    )
-    (both,) = add_call([keep_out, got_out], 1, after=(token,))
-    terms_out = exchange(both, (ZH, X))
+        inward_kernel,
+        16,
+        32,
+        scalars,
+        rows,
+        cols,
+        tiles,
+        (near_col, far_col),
+        (far_row,),
+    )
+    outward, token = spmm_call(
+        outward_kernel, 32, 16, scalars, rows, cols, tiles, (near_row, far_row), (token,), 1
+    )
+    both = fold_call(exchange(outward, CORE), 2)
+    terms_out = exchange(fold_call(exchange(both, X), 4), ZH)
     parts = add_call([keep, swap(send, YP, 1)], 4, cost=COST)
     got = [swap(part, YQ, bit) for part, bit in zip(parts[1:], (1, 2, 3))]
-    keep, send = add_call([parts[0], *got], 2)
+    keep, send = add_call([parts[0], *got], 2, cost=COST2)
     terms_in = [keep, swap(send, ZL, 1)]
     return pl.pallas_call(
         final_kernel,

time: 113 us -> 108 us (0.956)
  the two profiles are of different devices: /device:TPU:10 before, /device:TPU:8 now
where the time goes in v4:
time: 108 us
  starting transfers between devices  52.9 us (49%)
  blocking collectives  28.8 us (27%)
  waiting for transfers between devices  14 us (13%)
  Pallas kernels  8.21 us (8%)
  local copies, waits for them, and re-layouts  2.7 us (2%)
    ppermute x7, starting transfers between devices, swap(): return lax.ppermute(value, axis, [(i, i ^ bit) for i in range(size)])  26.8 us
    all_to_all x3, starting transfers between devices, exchange(): return lax.all_to_all(parts, axis, 0, 0, tiled=True)  26.2 us
    all_gather x1, blocking collectives, per_device(): near_row = lax.all_gather(near_row, YQ, axis=0, tiled=True)  17.9 us
    ppermute x7, waiting for transfers between devices, swap(): return lax.ppermute(value, axis, [(i, i ^ bit) for i in range(size)])  8.14 us
    all_to_all x3, waiting for transfers between devices, exchange(): return lax.all_to_all(parts, axis, 0, 0, tiled=True)  5.83 us
    all_gather x1, blocking collectives, per_device(): near_row = lax.all_gather(feats, ZL)  5.53 us
    all_to_all x1, blocking collectives, exchange(): return lax.all_to_all(parts, axis, 0, 0, tiled=True)  5.41 us
    pallas_call x2, Pallas kernels, spmm_call(): pl.pallas_call(functools.partial(kernel, len(parts)), out_shape=[part] *...  3.9 us
  transfers between devices with their start and end apart: 10, of which 4 were waited for; matrix products, arithmetic and copies ran while one was open for 0% of the time, Pallas kernels for 4%

profile of v4, /device:TPU:8, one launch (start us, length us, event | category | flops | bytes accessed | tf_op | source)
XLA Modules:
  0.0 107.6 jit_solution(5230161012983224902)
XLA Ops:
  0.0 5.5 %all-gather = bf16[256,256]{1,0:T(8,128)(2,1)S(1)} all-gather(bf16[128,256]{1,0:T(8,128)(2,1)} %feats.1), channel_id=2, replica_groups=mesh['zh'=4,'x'=4,'core'=2,'yq'=4,'yp'=2,'zl'=2] {'zl'}, dimensions={0}, use_global_device_ids=true | all-gather | bytes 196608 | tf_op jit(solution)/shard_map/all_gather | solution.py:236
  5.5 0.8 copy-done.1
  6.4 1.1 shard_map.92
  7.5 12.5 %all-to-all-start = ((bf16[16,128,256]{2,1,0:T(8,128)(2,1)}), bf16[16,128,256]{2,1,0:T(8,128)(2,1)S(1)}, u32[]{:S(2)}, u32[]{:S(2)}) async-start(bf16[16,128,256]{2,1,0:T(8,128)(2,1)} %shard_map.92), calls=%async_computation | async-start | bytes 2097152 | tf_op jit(solution)/shard_map/all_to_all | solution.py:222
  19.9 17.9 %all_gather.11.refs_0_ = bf16[8,128,256]{2,1,0:T(8,128)(2,1)S(1)} all-gather(bf16[2,128,256]{2,1,0:T(8,128)(2,1)S(1)} %bitcast.13), channel_id=1, replica_groups=mesh['zh'=4,'x'=4,'core'=2,'yq'=4,'yp'=2,'zl'=2] {'yq'}, dimensions={0}, use_global_device_ids=true | all-gather | bytes 655360 | tf_op jit(solution)/shard_map/all_gather | solution.py:238
  37.8 3.7 %collective-permute-start = (bf16[8,128,256]{2,1,0:T(8,128)(2,1)S(1)}, bf16[8,128,256]{2,1,0:T(8,128)(2,1)S(1)}, u32[]{:S(2)}, u32[]{:S(2)}) collective-permute-start(bf16[8,128,256]{2,1,0:T(8,128)(2,1)S(1)} %all_gather.11.refs_0_), channel_id=1, source_target_pairs={{0,2},{2,0},{1,3},{3,1},{4,6},{6,4},{5,7},{7,5},{8,10},{10,8},{9,1... | collective-permute-start | bytes 1572872 | tf_op jit(solution)/shard_map/ppermute | solution.py:227
  42.4 1.9 %collective-permute-start.1 = (bf16[16,128,256]{2,1,0:T(8,128)(2,1)S(1)}, bf16[16,128,256]{2,1,0:T(8,128)(2,1)S(1)}, u32[]{:S(2)}, u32[]{:S(2)}) collective-permute-start(bf16[16,128,256]{2,1,0:T(8,128)(2,1)S(1)} %shard_map.93.refs_0_), channel_id=1, source_target_pairs={{0,16},{16,0},{1,17},{17,1},{2,18},{18,2},{3,19},{19,3},{4,20},{20... | collective-permute-start | bytes 3145736 | tf_op jit(solution)/shard_map/ppermute | solution.py:227
  44.3 5.5 %collective-permute-done.value = bf16[8,128,256]{2,1,0:T(8,128)(2,1)S(1)} collective-permute-done((bf16[8,128,256]{2,1,0:T(8,128)(2,1)S(1)}, bf16[8,128,256]{2,1,0:T(8,128)(2,1)S(1)}, u32[]{:S(2)}, u32[]{:S(2)}) %collective-permute-start) | collective-permute-done | bytes 524320 | tf_op jit(solution)/shard_map/ppermute | solution.py:227
  49.9 1.8 %copy-done = bf16[1,1,96,128,128]{4,3,2,1,0:T(8,128)(2,1)S(1)} copy-done((bf16[1,1,96,128,128]{4,3,2,1,0:T(8,128)(2,1)S(1)}, bf16[1,1,96,128,128]{4,3,2,1,0:T(8,128)(2,1)}, u32[]{:S(2)}) %copy-start) | copy-done | bytes 3145752
  51.7 1.6 %shard_map.94 = (bf16[8,128,256]{2,1,0:T(8,128)(2,1)S(1)}, bf16[8,128,256]{2,1,0:T(8,128)(2,1)S(1)}, f32[8,128]{1,0:T(8,128)S(1)}) custom-call(s32[3]{0:T(128)S(1)} %pad_add_fusion.scalars, s32[96]{0:T(128)S(1)} %bitcast.15, s32[96]{0:T(128)S(1)} %bitcast.17, bf16[96,128,128]{2,1,0:T(8,128)(2,1)S(1)} %bitcast.10, ...), custom_call_target="tpu_custom_call" | custom-call | flops 805306368 | bytes 8388608 | tf_op jit(solution)/shard_map/pallas_call | solution.py:186
  53.4 3.6 %collective-permute-start.2 = (bf16[8,128,256]{2,1,0:T(8,128)(2,1)S(1)}, bf16[8,128,256]{2,1,0:T(8,128)(2,1)S(1)}, u32[]{:S(2)}, u32[]{:S(2)}) collective-permute-start(bf16[8,128,256]{2,1,0:T(8,128)(2,1)S(1)} %get-tuple-element.18), channel_id=1, source_target_pairs={{0,2},{2,0},{1,3},{3,1},{4,6},{6,4},{5,7},{7,5},{8,10},{10,8},{9,1... | collective-permute-start | bytes 1572872 | tf_op jit(solution)/shard_map/ppermute | solution.py:227
  57.0 2.3 %shard_map.95 = (bf16[32,128,256]{2,1,0:T(8,128)(2,1)S(1)}, f32[8,128]{1,0:T(8,128)}) custom-call(s32[3]{0:T(128)S(1)} %pad_add_fusion.scalars, s32[96]{0:T(128)S(1)} %bitcast.16, s32[96]{0:T(128)S(1)} %bitcast.18, bf16[96,128,128]{2,1,0:T(8,128)(2,1)S(1)} %bitcast.11, bf16[8,128,256]{2,1,0:T(8,128)(2,1)S(1)} %all_gather.11.refs_0_, ...), custom_call_target="tpu_custom_call" | custom-call | flops 805306368 | bytes 8388608 | tf_op jit(solution)/shard_map/pallas_call | solution.py:186
  59.3 5.4 %all_to_all.20.parts = bf16[32,128,256]{2,1,0:T(8,128)(2,1)S(1)} all-to-all(bf16[32,128,256]{2,1,0:T(8,128)(2,1)S(1)} %get-tuple-element.16), channel_id=1, replica_groups=mesh['zh'=4,'x'=4,'core'=2,'yq'=4,'yp'=2,'zl'=2] {'core'}, dimensions={0} | all-to-all | bytes 4194304 | tf_op jit(solution)/shard_map/all_to_all | solution.py:222
  64.7 1.2 %shard_map.96 = bf16[16,128,256]{2,1,0:T(8,128)(2,1)} custom-call(bf16[32,128,256]{2,1,0:T(8,128)(2,1)S(1)} %all_to_all.20.parts), custom_call_target="tpu_custom_call" | custom-call | flops 1048576 | bytes 3145728 | tf_op jit(solution)/shard_map/pallas_call | solution.py:171
  65.9 6.0 %all-to-all-start.2 = ((bf16[16,128,256]{2,1,0:T(8,128)(2,1)}), bf16[16,128,256]{2,1,0:T(8,128)(2,1)S(1)}, u32[]{:S(2)}, u32[]{:S(2)}) async-start(bf16[16,128,256]{2,1,0:T(8,128)(2,1)} %shard_map.96), calls=%async_computation.2 | async-start | bytes 2097152 | tf_op jit(solution)/shard_map/all_to_all | solution.py:222
  72.1 3.2 %collective-permute-start.3 = (bf16[2,128,256]{2,1,0:T(8,128)(2,1)S(1)}, bf16[2,128,256]{2,1,0:T(8,128)(2,1)S(1)}, u32[]{:S(2)}, u32[]{:S(2)}) collective-permute-start(bf16[2,128,256]{2,1,0:T(8,128)(2,1)S(1)} %get-tuple-element.20), channel_id=1, source_target_pairs={{0,4},{4,0},{8,12},{12,8},{1,5},{5,1},{9,13},{13,9},{2,6},{6,2},{1... | collective-permute-start | bytes 393224 | tf_op jit(solution)/shard_map/ppermute | solution.py:227
  75.3 5.7 %collective-permute-start.4 = (bf16[2,128,256]{2,1,0:T(8,128)(2,1)S(1)}, bf16[2,128,256]{2,1,0:T(8,128)(2,1)S(1)}, u32[]{:S(2)}, u32[]{:S(2)}) collective-permute-start(bf16[2,128,256]{2,1,0:T(8,128)(2,1)S(1)} %get-tuple-element.21), channel_id=1, source_target_pairs={{0,8},{4,12},{8,0},{12,4},{1,9},{5,13},{9,1},{13,5},{2,10},{6,14},... | collective-permute-start | bytes 393224 | tf_op jit(solution)/shard_map/ppermute | solution.py:227
  81.0 3.3 %collective-permute-start.5 = (bf16[2,128,256]{2,1,0:T(8,128)(2,1)S(1)}, bf16[2,128,256]{2,1,0:T(8,128)(2,1)S(1)}, u32[]{:S(2)}, u32[]{:S(2)}) collective-permute-start(bf16[2,128,256]{2,1,0:T(8,128)(2,1)S(1)} %get-tuple-element.22), channel_id=1, source_target_pairs={{0,12},{4,8},{8,4},{12,0},{1,13},{5,9},{9,5},{13,1},{2,14},{6,10},... | collective-permute-start | bytes 393224 | tf_op jit(solution)/shard_map/ppermute | solution.py:227
  84.3 3.0 %all-to-all-done.2.parts = bf16[16,128,256]{2,1,0:T(8,128)(2,1)S(1)} async-done(((bf16[16,128,256]{2,1,0:T(8,128)(2,1)}), bf16[16,128,256]{2,1,0:T(8,128)(2,1)S(1)}, u32[]{:S(2)}, u32[]{:S(2)}) %all-to-all-start.2) | async-done | bytes 1048608 | tf_op jit(solution)/shard_map/all_to_all | solution.py:222
  88.2 7.7 %all-to-all-start.3 = ((bf16[4,128,256]{2,1,0:T(8,128)(2,1)}), bf16[4,128,256]{2,1,0:T(8,128)(2,1)S(1)}, u32[]{:S(2)}, u32[]{:S(2)}) async-start(bf16[4,128,256]{2,1,0:T(8,128)(2,1)} %shard_map.97), calls=%async_computation.3 | async-start | bytes 524288 | tf_op jit(solution)/shard_map/all_to_all | solution.py:222
  96.0 5.3 %collective-permute-start.6 = (bf16[1,128,256]{2,1,0:T(8,128)(2,1)S(1)}, bf16[1,128,256]{2,1,0:T(8,128)(2,1)S(1)}, u32[]{:S(2)}, u32[]{:S(2)}) collective-permute-start(bf16[1,128,256]{2,1,0:T(8,128)(2,1)S(1)} %get-tuple-element.24), channel_id=1, source_target_pairs={{0,1},{1,0},{2,3},{3,2},{4,5},{5,4},{6,7},{7,6},{8,9},{9,8},{10,11... | collective-permute-start | bytes 196616 | tf_op jit(solution)/shard_map/ppermute | solution.py:227
  101.3 2.6 %collective-permute-done.6.refs_1_ = bf16[1,128,256]{2,1,0:T(8,128)(2,1)S(1)} collective-permute-done((bf16[1,128,256]{2,1,0:T(8,128)(2,1)S(1)}, bf16[1,128,256]{2,1,0:T(8,128)(2,1)S(1)}, u32[]{:S(2)}, u32[]{:S(2)}) %collective-permute-start.6) | collective-permute-done | bytes 65568 | tf_op jit(solution)/shard_map/ppermute | solution.py:227
  103.9 2.8 %all-to-all-done.3.terms_out = bf16[4,128,256]{2,1,0:T(8,128)(2,1)S(1)} async-done(((bf16[4,128,256]{2,1,0:T(8,128)(2,1)}), bf16[4,128,256]{2,1,0:T(8,128)(2,1)S(1)}, u32[]{:S(2)}, u32[]{:S(2)}) %all-to-all-start.3) | async-done | bytes 262176 | tf_op jit(solution)/shard_map/all_to_all | solution.py:222
  106.7 0.9 shard_map.100
  (28 shorter events, 1.3 us)
Async XLA Ops:
  5.5 0.8 copy-start.1
  7.5 34.8 %all-to-all-start = ((bf16[16,128,256]{2,1,0:T(8,128)(2,1)}), bf16[16,128,256]{2,1,0:T(8,128)(2,1)S(1)}, u32[]{:S(2)}, u32[]{:S(2)}) async-start(bf16[16,128,256]{2,1,0:T(8,128)(2,1)} %shard_map.92), calls=%async_computation | async-start | bytes 2097152 | tf_op jit(solution)/shard_map/all_to_all | solution.py:222
  37.8 12.0 %collective-permute-start = (bf16[8,128,256]{2,1,0:T(8,128)(2,1)S(1)}, bf16[8,128,256]{2,1,0:T(8,128)(2,1)S(1)}, u32[]{:S(2)}, u32[]{:S(2)}) collective-permute-start(bf16[8,128,256]{2,1,0:T(8,128)(2,1)S(1)} %all_gather.11.refs_0_), channel_id=1, source_target_pairs={{0,2},{2,0},{1,3},{3,1},{4,6},{6,4},{5,7},{7,5},{8,10},{10,8},{9,1... | collective-permute-start | bytes 1572872 | tf_op jit(solution)/shard_map/ppermute | solution.py:227
  42.4 7.5 %copy-start.6 = (s32[1,1,96]{2,1,0:T(1,128)S(1)}, s32[1,1,96]{2,1,0:T(1,128)}, u32[]{:S(2)}) copy-start(s32[1,1,96]{2,1,0:T(1,128)} %param.11) | copy-start | bytes 1156
  42.4 7.5 %copy-start.7 = (s32[1,1,96]{2,1,0:T(1,128)S(1)}, s32[1,1,96]{2,1,0:T(1,128)}, u32[]{:S(2)}) copy-start(s32[1,1,96]{2,1,0:T(1,128)} %param.12) | copy-start | bytes 1156
  42.4 7.5 %collective-permute-start.1 = (bf16[16,128,256]{2,1,0:T(8,128)(2,1)S(1)}, bf16[16,128,256]{2,1,0:T(8,128)(2,1)S(1)}, u32[]{:S(2)}, u32[]{:S(2)}) collective-permute-start(bf16[16,128,256]{2,1,0:T(8,128)(2,1)S(1)} %shard_map.93.refs_0_), channel_id=1, source_target_pairs={{0,16},{16,0},{1,17},{17,1},{2,18},{18,2},{3,19},{19,3},{4,20},{20... | collective-permute-start | bytes 3145736 | tf_op jit(solution)/shard_map/ppermute | solution.py:227
  49.8 1.9 %copy-start = (bf16[1,1,96,128,128]{4,3,2,1,0:T(8,128)(2,1)S(1)}, bf16[1,1,96,128,128]{4,3,2,1,0:T(8,128)(2,1)}, u32[]{:S(2)}) copy-start(bf16[1,1,96,128,128]{4,3,2,1,0:T(8,128)(2,1)} %param.10) | copy-start | bytes 9437188
  53.4 18.5 %collective-permute-start.2 = (bf16[8,128,256]{2,1,0:T(8,128)(2,1)S(1)}, bf16[8,128,256]{2,1,0:T(8,128)(2,1)S(1)}, u32[]{:S(2)}, u32[]{:S(2)}) collective-permute-start(bf16[8,128,256]{2,1,0:T(8,128)(2,1)S(1)} %get-tuple-element.18), channel_id=1, source_target_pairs={{0,2},{2,0},{1,3},{3,1},{4,6},{6,4},{5,7},{7,5},{8,10},{10,8},{9,1... | collective-permute-start | bytes 1572872 | tf_op jit(solution)/shard_map/ppermute | solution.py:227
  65.9 21.4 %all-to-all-start.2 = ((bf16[16,128,256]{2,1,0:T(8,128)(2,1)}), bf16[16,128,256]{2,1,0:T(8,128)(2,1)S(1)}, u32[]{:S(2)}, u32[]{:S(2)}) async-start(bf16[16,128,256]{2,1,0:T(8,128)(2,1)} %shard_map.96), calls=%async_computation.2 | async-start | bytes 2097152 | tf_op jit(solution)/shard_map/all_to_all | solution.py:222
  72.1 23.8 %collective-permute-start.3 = (bf16[2,128,256]{2,1,0:T(8,128)(2,1)S(1)}, bf16[2,128,256]{2,1,0:T(8,128)(2,1)S(1)}, u32[]{:S(2)}, u32[]{:S(2)}) collective-permute-start(bf16[2,128,256]{2,1,0:T(8,128)(2,1)S(1)} %get-tuple-element.20), channel_id=1, source_target_pairs={{0,4},{4,0},{8,12},{12,8},{1,5},{5,1},{9,13},{13,9},{2,6},{6,2},{1... | collective-permute-start | bytes 393224 | tf_op jit(solution)/shard_map/ppermute | solution.py:227
  75.3 20.5 %collective-permute-start.4 = (bf16[2,128,256]{2,1,0:T(8,128)(2,1)S(1)}, bf16[2,128,256]{2,1,0:T(8,128)(2,1)S(1)}, u32[]{:S(2)}, u32[]{:S(2)}) collective-permute-start(bf16[2,128,256]{2,1,0:T(8,128)(2,1)S(1)} %get-tuple-element.21), channel_id=1, source_target_pairs={{0,8},{4,12},{8,0},{12,4},{1,9},{5,13},{9,1},{13,5},{2,10},{6,14},... | collective-permute-start | bytes 393224 | tf_op jit(solution)/shard_map/ppermute | solution.py:227
  81.0 14.9 %collective-permute-start.5 = (bf16[2,128,256]{2,1,0:T(8,128)(2,1)S(1)}, bf16[2,128,256]{2,1,0:T(8,128)(2,1)S(1)}, u32[]{:S(2)}, u32[]{:S(2)}) collective-permute-start(bf16[2,128,256]{2,1,0:T(8,128)(2,1)S(1)} %get-tuple-element.22), channel_id=1, source_target_pairs={{0,12},{4,8},{8,4},{12,0},{1,13},{5,9},{9,5},{13,1},{2,14},{6,10},... | collective-permute-start | bytes 393224 | tf_op jit(solution)/shard_map/ppermute | solution.py:227
  88.2 18.5 %all-to-all-start.3 = ((bf16[4,128,256]{2,1,0:T(8,128)(2,1)}), bf16[4,128,256]{2,1,0:T(8,128)(2,1)S(1)}, u32[]{:S(2)}, u32[]{:S(2)}) async-start(bf16[4,128,256]{2,1,0:T(8,128)(2,1)} %shard_map.97), calls=%async_computation.3 | async-start | bytes 524288 | tf_op jit(solution)/shard_map/all_to_all | solution.py:222
  95.9 10.8 %copy-start.2 = (bf16[128,256]{1,0:T(8,128)(2,1)S(1)}, bf16[128,256]{1,0:T(8,128)(2,1)}, u32[]{:S(2)}) copy-start(bf16[128,256]{1,0:T(8,128)(2,1)} %feats.1) | copy-start | bytes 196612
  95.9 10.8 %copy-start.3 = (bf16[256,256]{1,0:T(8,128)(2,1)S(1)}, bf16[256,256]{1,0:T(8,128)(2,1)}, u32[]{:S(2)}) copy-start(bf16[256,256]{1,0:T(8,128)(2,1)} %w_self.1) | copy-start | bytes 393220
  95.9 10.8 %copy-start.4 = (bf16[256,256]{1,0:T(8,128)(2,1)S(1)}, bf16[256,256]{1,0:T(8,128)(2,1)}, u32[]{:S(2)}) copy-start(bf16[256,256]{1,0:T(8,128)(2,1)} %w_in.1) | copy-start | bytes 393220
  95.9 10.8 %copy-start.5 = (bf16[256,256]{1,0:T(8,128)(2,1)S(1)}, bf16[256,256]{1,0:T(8,128)(2,1)}, u32[]{:S(2)}) copy-start(bf16[256,256]{1,0:T(8,128)(2,1)} %w_out.1) | copy-start | bytes 393220
  95.9 10.8 %copy-start.8 = (f32[256]{0:T(256)S(1)}, f32[256]{0:T(256)}, u32[]{:S(2)}) copy-start(f32[256]{0:T(256)} %param.17) | copy-start | bytes 3076
  96.0 7.9 %collective-permute-start.6 = (bf16[1,128,256]{2,1,0:T(8,128)(2,1)S(1)}, bf16[1,128,256]{2,1,0:T(8,128)(2,1)S(1)}, u32[]{:S(2)}, u32[]{:S(2)}) collective-permute-start(bf16[1,128,256]{2,1,0:T(8,128)(2,1)S(1)} %get-tuple-element.24), channel_id=1, source_target_pairs={{0,1},{1,0},{2,3},{3,2},{4,5},{5,4},{6,7},{7,6},{8,9},{9,8},{10,11... | collective-permute-start | bytes 196616 | tf_op jit(solution)/shard_map/ppermute | solution.py:227

commit v5 on v4

--- a/solution.py
+++ b/solution.py
@@ -8,7 +8,7 @@
 from jax.sharding import Mesh, PartitionSpec as P
 
 ZH, X, CORE, YQ, YP, ZL = "zh", "x", "core", "yq", "yp", "zl"
-UNROLL = 32
+UNROLL = 48
 COST = 20000
 COST2 = 40000
 TIE_COST = 10**11
@@ -237,7 +237,6 @@
     near_col = exchange(copies_call(feats[None], 16, near_row), (ZH, X))
     near_row = lax.all_gather(near_row, YQ, axis=0, tiled=True)
     far_row = tie_call(swap(near_row, YP, 1), (), TIE_COST)
-    near_col = tie_call(near_col, (near_row,))
     far_col = swap(near_col, CORE, 1)
 
     keep, send, token = spmm_call(

time: 108 us -> 107 us (level)
  the two profiles are of different devices: /device:TPU:8 before, /device:TPU:24 now
where the time goes in v5:
time: 107 us; the launch traced here: 106 us
  starting transfers between devices  50.1 us (47%)
  blocking collectives  26.6 us (25%)
  waiting for transfers between devices  16.9 us (16%)
  Pallas kernels  8.69 us (8%)
  local copies, waits for them, and re-layouts  2.7 us (3%)
    ppermute x7, starting transfers between devices, swap(): return lax.ppermute(value, axis, [(i, i ^ bit) for i in range(size)])  25.3 us
    all_to_all x3, starting transfers between devices, exchange(): return lax.all_to_all(parts, axis, 0, 0, tiled=True)  24.8 us
    all_gather x1, blocking collectives, per_device(): near_row = lax.all_gather(near_row, YQ, axis=0, tiled=True)  15.7 us
    all_to_all x3, waiting for transfers between devices, exchange(): return lax.all_to_all(parts, axis, 0, 0, tiled=True)  8.85 us
    ppermute x7, waiting for transfers between devices, swap(): return lax.ppermute(value, axis, [(i, i ^ bit) for i in range(size)])  8.03 us
    all_gather x1, blocking collectives, per_device(): near_row = lax.all_gather(feats, ZL)  5.53 us
    all_to_all x1, blocking collectives, exchange(): return lax.all_to_all(parts, axis, 0, 0, tiled=True)  5.41 us
    pallas_call x2, Pallas kernels, spmm_call(): pl.pallas_call(functools.partial(kernel, len(parts)), out_shape=[part] *...  4.46 us
  transfers between devices with their start and end apart: 10, of which 5 were waited for; matrix products, arithmetic and copies ran while one was open for 0% of the time, Pallas kernels for 5%

profile of v5, /device:TPU:24, one launch (start us, length us, event | category | flops | bytes accessed | tf_op | source)
XLA Modules:
  0.0 105.9 jit_solution(7540403886253641345)
XLA Ops:
  0.0 5.5 %all-gather = bf16[256,256]{1,0:T(8,128)(2,1)S(1)} all-gather(bf16[128,256]{1,0:T(8,128)(2,1)} %feats.1), channel_id=2, replica_groups=mesh['zh'=4,'x'=4,'core'=2,'yq'=4,'yp'=2,'zl'=2] {'zl'}, dimensions={0}, use_global_device_ids=true | all-gather | bytes 196608 | tf_op jit(solution)/shard_map/all_gather | solution.py:236
  6.4 1.1 %shard_map.92 = bf16[16,128,256]{2,1,0:T(8,128)(2,1)} custom-call(bf16[1,128,256]{2,1,0:T(8,128)(2,1)S(1)} %bitcast.14, bf16[2,128,256]{2,1,0:T(8,128)(2,1)S(1)} %bitcast.12), custom_call_target="tpu_custom_call" | custom-call | bytes 1114112 | tf_op jit(solution)/shard_map/pallas_call | solution.py:133
  7.5 12.5 %all-to-all-start = ((bf16[16,128,256]{2,1,0:T(8,128)(2,1)}), bf16[16,128,256]{2,1,0:T(8,128)(2,1)S(1)}, u32[]{:S(2)}, u32[]{:S(2)}) async-start(bf16[16,128,256]{2,1,0:T(8,128)(2,1)} %shard_map.92), calls=%async_computation | async-start | bytes 2097152 | tf_op jit(solution)/shard_map/all_to_all | solution.py:222
  19.9 15.7 %all_gather.11.refs_0_ = bf16[8,128,256]{2,1,0:T(8,128)(2,1)S(1)} all-gather(bf16[2,128,256]{2,1,0:T(8,128)(2,1)S(1)} %bitcast.13), channel_id=1, replica_groups=mesh['zh'=4,'x'=4,'core'=2,'yq'=4,'yp'=2,'zl'=2] {'yq'}, dimensions={0}, use_global_device_ids=true | all-gather | bytes 655360 | tf_op jit(solution)/shard_map/all_gather | solution.py:238
  35.6 3.7 %collective-permute-start = (bf16[8,128,256]{2,1,0:T(8,128)(2,1)S(1)}, bf16[8,128,256]{2,1,0:T(8,128)(2,1)S(1)}, u32[]{:S(2)}, u32[]{:S(2)}) collective-permute-start(bf16[8,128,256]{2,1,0:T(8,128)(2,1)S(1)} %all_gather.11.refs_0_), channel_id=1, source_target_pairs={{0,2},{2,0},{1,3},{3,1},{4,6},{6,4},{5,7},{7,5},{8,10},{10,8},{9,1... | collective-permute-start | bytes 1572872 | tf_op jit(solution)/shard_map/ppermute | solution.py:227
  40.1 2.0 %all-to-all-done.refs_0_ = bf16[16,128,256]{2,1,0:T(8,128)(2,1)S(1)} async-done(((bf16[16,128,256]{2,1,0:T(8,128)(2,1)}), bf16[16,128,256]{2,1,0:T(8,128)(2,1)S(1)}, u32[]{:S(2)}, u32[]{:S(2)}) %all-to-all-start) | async-done | bytes 1048608 | tf_op jit(solution)/shard_map/all_to_all | solution.py:222
  42.1 1.9 %collective-permute-start.1 = (bf16[16,128,256]{2,1,0:T(8,128)(2,1)S(1)}, bf16[16,128,256]{2,1,0:T(8,128)(2,1)S(1)}, u32[]{:S(2)}, u32[]{:S(2)}) collective-permute-start(bf16[16,128,256]{2,1,0:T(8,128)(2,1)S(1)} %all-to-all-done.refs_0_), channel_id=1, source_target_pairs={{0,16},{16,0},{1,17},{17,1},{2,18},{18,2},{3,19},{19,3},{4,20},{20... | collective-permute-start | bytes 3145736 | tf_op jit(solution)/shard_map/ppermute | solution.py:227
  44.0 4.4 %collective-permute-done.value = bf16[8,128,256]{2,1,0:T(8,128)(2,1)S(1)} collective-permute-done((bf16[8,128,256]{2,1,0:T(8,128)(2,1)S(1)}, bf16[8,128,256]{2,1,0:T(8,128)(2,1)S(1)}, u32[]{:S(2)}, u32[]{:S(2)}) %collective-permute-start) | collective-permute-done | bytes 524320 | tf_op jit(solution)/shard_map/ppermute | solution.py:227
  48.5 1.8 %copy-done = bf16[1,1,96,128,128]{4,3,2,1,0:T(8,128)(2,1)S(1)} copy-done((bf16[1,1,96,128,128]{4,3,2,1,0:T(8,128)(2,1)S(1)}, bf16[1,1,96,128,128]{4,3,2,1,0:T(8,128)(2,1)}, u32[]{:S(2)}) %copy-start) | copy-done | bytes 3145752
  50.3 1.9 %shard_map.93 = (bf16[8,128,256]{2,1,0:T(8,128)(2,1)S(1)}, bf16[8,128,256]{2,1,0:T(8,128)(2,1)S(1)}, f32[8,128]{1,0:T(8,128)S(1)}) custom-call(s32[3]{0:T(128)S(1)} %pad_add_fusion.scalars, s32[96]{0:T(128)S(1)} %bitcast.15, s32[96]{0:T(128)S(1)} %bitcast.17, bf16[96,128,128]{2,1,0:T(8,128)(2,1)S(1)} %bitcast.10, ...), custom_call_target="tpu_custom_call" | custom-call | flops 805306368 | bytes 8388608 | tf_op jit(solution)/shard_map/pallas_call | solution.py:186
  52.2 3.6 %collective-permute-start.2 = (bf16[8,128,256]{2,1,0:T(8,128)(2,1)S(1)}, bf16[8,128,256]{2,1,0:T(8,128)(2,1)S(1)}, u32[]{:S(2)}, u32[]{:S(2)}) collective-permute-start(bf16[8,128,256]{2,1,0:T(8,128)(2,1)S(1)} %get-tuple-element.18), channel_id=1, source_target_pairs={{0,2},{2,0},{1,3},{3,1},{4,6},{6,4},{5,7},{7,5},{8,10},{10,8},{9,1... | collective-permute-start | bytes 1572872 | tf_op jit(solution)/shard_map/ppermute | solution.py:227
  55.9 2.5 %shard_map.94 = (bf16[32,128,256]{2,1,0:T(8,128)(2,1)S(1)}, f32[8,128]{1,0:T(8,128)}) custom-call(s32[3]{0:T(128)S(1)} %pad_add_fusion.scalars, s32[96]{0:T(128)S(1)} %bitcast.16, s32[96]{0:T(128)S(1)} %bitcast.18, bf16[96,128,128]{2,1,0:T(8,128)(2,1)S(1)} %bitcast.11, bf16[8,128,256]{2,1,0:T(8,128)(2,1)S(1)} %all_gather.11.refs_0_, ...), custom_call_target="tpu_custom_call" | custom-call | flops 805306368 | bytes 8388608 | tf_op jit(solution)/shard_map/pallas_call | solution.py:186
  58.4 5.4 %all_to_all.20.parts = bf16[32,128,256]{2,1,0:T(8,128)(2,1)S(1)} all-to-all(bf16[32,128,256]{2,1,0:T(8,128)(2,1)S(1)} %get-tuple-element.16), channel_id=1, replica_groups=mesh['zh'=4,'x'=4,'core'=2,'yq'=4,'yp'=2,'zl'=2] {'core'}, dimensions={0} | all-to-all | bytes 4194304 | tf_op jit(solution)/shard_map/all_to_all | solution.py:222
  63.8 1.2 %shard_map.95 = bf16[16,128,256]{2,1,0:T(8,128)(2,1)} custom-call(bf16[32,128,256]{2,1,0:T(8,128)(2,1)S(1)} %all_to_all.20.parts), custom_call_target="tpu_custom_call" | custom-call | flops 1048576 | bytes 3145728 | tf_op jit(solution)/shard_map/pallas_call | solution.py:171
  65.1 5.7 %all-to-all-start.2 = ((bf16[16,128,256]{2,1,0:T(8,128)(2,1)}), bf16[16,128,256]{2,1,0:T(8,128)(2,1)S(1)}, u32[]{:S(2)}, u32[]{:S(2)}) async-start(bf16[16,128,256]{2,1,0:T(8,128)(2,1)} %shard_map.95), calls=%async_computation.2 | async-start | bytes 2097152 | tf_op jit(solution)/shard_map/all_to_all | solution.py:222
  70.9 2.6 %collective-permute-start.3 = (bf16[2,128,256]{2,1,0:T(8,128)(2,1)S(1)}, bf16[2,128,256]{2,1,0:T(8,128)(2,1)S(1)}, u32[]{:S(2)}, u32[]{:S(2)}) collective-permute-start(bf16[2,128,256]{2,1,0:T(8,128)(2,1)S(1)} %get-tuple-element.20), channel_id=1, source_target_pairs={{0,4},{4,0},{8,12},{12,8},{1,5},{5,1},{9,13},{13,9},{2,6},{6,2},{1... | collective-permute-start | bytes 393224 | tf_op jit(solution)/shard_map/ppermute | solution.py:227
  73.5 5.1 %collective-permute-start.4 = (bf16[2,128,256]{2,1,0:T(8,128)(2,1)S(1)}, bf16[2,128,256]{2,1,0:T(8,128)(2,1)S(1)}, u32[]{:S(2)}, u32[]{:S(2)}) collective-permute-start(bf16[2,128,256]{2,1,0:T(8,128)(2,1)S(1)} %get-tuple-element.21), channel_id=1, source_target_pairs={{0,8},{4,12},{8,0},{12,4},{1,9},{5,13},{9,1},{13,5},{2,10},{6,14},... | collective-permute-start | bytes 393224 | tf_op jit(solution)/shard_map/ppermute | solution.py:227
  78.6 4.5 %collective-permute-start.5 = (bf16[2,128,256]{2,1,0:T(8,128)(2,1)S(1)}, bf16[2,128,256]{2,1,0:T(8,128)(2,1)S(1)}, u32[]{:S(2)}, u32[]{:S(2)}) collective-permute-start(bf16[2,128,256]{2,1,0:T(8,128)(2,1)S(1)} %get-tuple-element.22), channel_id=1, source_target_pairs={{0,12},{4,8},{8,4},{12,0},{1,13},{5,9},{9,5},{13,1},{2,14},{6,10},... | collective-permute-start | bytes 393224 | tf_op jit(solution)/shard_map/ppermute | solution.py:227
  83.2 3.0 %all-to-all-done.2.parts = bf16[16,128,256]{2,1,0:T(8,128)(2,1)S(1)} async-done(((bf16[16,128,256]{2,1,0:T(8,128)(2,1)}), bf16[16,128,256]{2,1,0:T(8,128)(2,1)S(1)}, u32[]{:S(2)}, u32[]{:S(2)}) %all-to-all-start.2) | async-done | bytes 1048608 | tf_op jit(solution)/shard_map/all_to_all | solution.py:222
  87.0 6.6 %all-to-all-start.3 = ((bf16[4,128,256]{2,1,0:T(8,128)(2,1)}), bf16[4,128,256]{2,1,0:T(8,128)(2,1)S(1)}, u32[]{:S(2)}, u32[]{:S(2)}) async-start(bf16[4,128,256]{2,1,0:T(8,128)(2,1)} %shard_map.96), calls=%async_computation.3 | async-start | bytes 524288 | tf_op jit(solution)/shard_map/all_to_all | solution.py:222
  93.7 3.8 %collective-permute-start.6 = (bf16[1,128,256]{2,1,0:T(8,128)(2,1)S(1)}, bf16[1,128,256]{2,1,0:T(8,128)(2,1)S(1)}, u32[]{:S(2)}, u32[]{:S(2)}) collective-permute-start(bf16[1,128,256]{2,1,0:T(8,128)(2,1)S(1)} %get-tuple-element.24), channel_id=1, source_target_pairs={{0,1},{1,0},{2,3},{3,2},{4,5},{5,4},{6,7},{7,6},{8,9},{9,8},{10,11... | collective-permute-start | bytes 196616 | tf_op jit(solution)/shard_map/ppermute | solution.py:227
  97.5 3.6 %collective-permute-done.6.refs_1_ = bf16[1,128,256]{2,1,0:T(8,128)(2,1)S(1)} collective-permute-done((bf16[1,128,256]{2,1,0:T(8,128)(2,1)S(1)}, bf16[1,128,256]{2,1,0:T(8,128)(2,1)S(1)}, u32[]{:S(2)}, u32[]{:S(2)}) %collective-permute-start.6) | collective-permute-done | bytes 65568 | tf_op jit(solution)/shard_map/ppermute | solution.py:227
  101.1 3.9 %all-to-all-done.3.terms_out = bf16[4,128,256]{2,1,0:T(8,128)(2,1)S(1)} async-done(((bf16[4,128,256]{2,1,0:T(8,128)(2,1)}), bf16[4,128,256]{2,1,0:T(8,128)(2,1)S(1)}, u32[]{:S(2)}, u32[]{:S(2)}) %all-to-all-start.3) | async-done | bytes 262176 | tf_op jit(solution)/shard_map/all_to_all | solution.py:222
  105.0 0.9 shard_map.99
  (27 shorter events, 2.0 us)
Async XLA Ops:
  5.5 0.8 copy-start.1
  7.5 34.6 %all-to-all-start = ((bf16[16,128,256]{2,1,0:T(8,128)(2,1)}), bf16[16,128,256]{2,1,0:T(8,128)(2,1)S(1)}, u32[]{:S(2)}, u32[]{:S(2)}) async-start(bf16[16,128,256]{2,1,0:T(8,128)(2,1)} %shard_map.92), calls=%async_computation | async-start | bytes 2097152 | tf_op jit(solution)/shard_map/all_to_all | solution.py:222
  35.6 12.8 %collective-permute-start = (bf16[8,128,256]{2,1,0:T(8,128)(2,1)S(1)}, bf16[8,128,256]{2,1,0:T(8,128)(2,1)S(1)}, u32[]{:S(2)}, u32[]{:S(2)}) collective-permute-start(bf16[8,128,256]{2,1,0:T(8,128)(2,1)S(1)} %all_gather.11.refs_0_), channel_id=1, source_target_pairs={{0,2},{2,0},{1,3},{3,1},{4,6},{6,4},{5,7},{7,5},{8,10},{10,8},{9,1... | collective-permute-start | bytes 1572872 | tf_op jit(solution)/shard_map/ppermute | solution.py:227
  40.1 8.4 %copy-start.6 = (s32[1,1,96]{2,1,0:T(1,128)S(1)}, s32[1,1,96]{2,1,0:T(1,128)}, u32[]{:S(2)}) copy-start(s32[1,1,96]{2,1,0:T(1,128)} %param.11) | copy-start | bytes 1156
  40.1 8.4 %copy-start.7 = (s32[1,1,96]{2,1,0:T(1,128)S(1)}, s32[1,1,96]{2,1,0:T(1,128)}, u32[]{:S(2)}) copy-start(s32[1,1,96]{2,1,0:T(1,128)} %param.12) | copy-start | bytes 1156
  42.1 6.4 %collective-permute-start.1 = (bf16[16,128,256]{2,1,0:T(8,128)(2,1)S(1)}, bf16[16,128,256]{2,1,0:T(8,128)(2,1)S(1)}, u32[]{:S(2)}, u32[]{:S(2)}) collective-permute-start(bf16[16,128,256]{2,1,0:T(8,128)(2,1)S(1)} %all-to-all-done.refs_0_), channel_id=1, source_target_pairs={{0,16},{16,0},{1,17},{17,1},{2,18},{18,2},{3,19},{19,3},{4,20},{20... | collective-permute-start | bytes 3145736 | tf_op jit(solution)/shard_map/ppermute | solution.py:227
  48.4 1.9 %copy-start = (bf16[1,1,96,128,128]{4,3,2,1,0:T(8,128)(2,1)S(1)}, bf16[1,1,96,128,128]{4,3,2,1,0:T(8,128)(2,1)}, u32[]{:S(2)}) copy-start(bf16[1,1,96,128,128]{4,3,2,1,0:T(8,128)(2,1)} %param.10) | copy-start | bytes 9437188
  52.2 18.6 %collective-permute-start.2 = (bf16[8,128,256]{2,1,0:T(8,128)(2,1)S(1)}, bf16[8,128,256]{2,1,0:T(8,128)(2,1)S(1)}, u32[]{:S(2)}, u32[]{:S(2)}) collective-permute-start(bf16[8,128,256]{2,1,0:T(8,128)(2,1)S(1)} %get-tuple-element.18), channel_id=1, source_target_pairs={{0,2},{2,0},{1,3},{3,1},{4,6},{6,4},{5,7},{7,5},{8,10},{10,8},{9,1... | collective-permute-start | bytes 1572872 | tf_op jit(solution)/shard_map/ppermute | solution.py:227
  65.1 21.1 %all-to-all-start.2 = ((bf16[16,128,256]{2,1,0:T(8,128)(2,1)}), bf16[16,128,256]{2,1,0:T(8,128)(2,1)S(1)}, u32[]{:S(2)}, u32[]{:S(2)}) async-start(bf16[16,128,256]{2,1,0:T(8,128)(2,1)} %shard_map.95), calls=%async_computation.2 | async-start | bytes 2097152 | tf_op jit(solution)/shard_map/all_to_all | solution.py:222
  70.9 22.7 %collective-permute-start.3 = (bf16[2,128,256]{2,1,0:T(8,128)(2,1)S(1)}, bf16[2,128,256]{2,1,0:T(8,128)(2,1)S(1)}, u32[]{:S(2)}, u32[]{:S(2)}) collective-permute-start(bf16[2,128,256]{2,1,0:T(8,128)(2,1)S(1)} %get-tuple-element.20), channel_id=1, source_target_pairs={{0,4},{4,0},{8,12},{12,8},{1,5},{5,1},{9,13},{13,9},{2,6},{6,2},{1... | collective-permute-start | bytes 393224 | tf_op jit(solution)/shard_map/ppermute | solution.py:227
  73.5 20.0 %collective-permute-start.4 = (bf16[2,128,256]{2,1,0:T(8,128)(2,1)S(1)}, bf16[2,128,256]{2,1,0:T(8,128)(2,1)S(1)}, u32[]{:S(2)}, u32[]{:S(2)}) collective-permute-start(bf16[2,128,256]{2,1,0:T(8,128)(2,1)S(1)} %get-tuple-element.21), channel_id=1, source_target_pairs={{0,8},{4,12},{8,0},{12,4},{1,9},{5,13},{9,1},{13,5},{2,10},{6,14},... | collective-permute-start | bytes 393224 | tf_op jit(solution)/shard_map/ppermute | solution.py:227
  78.6 15.0 %collective-permute-start.5 = (bf16[2,128,256]{2,1,0:T(8,128)(2,1)S(1)}, bf16[2,128,256]{2,1,0:T(8,128)(2,1)S(1)}, u32[]{:S(2)}, u32[]{:S(2)}) collective-permute-start(bf16[2,128,256]{2,1,0:T(8,128)(2,1)S(1)} %get-tuple-element.22), channel_id=1, source_target_pairs={{0,12},{4,8},{8,4},{12,0},{1,13},{5,9},{9,5},{13,1},{2,14},{6,10},... | collective-permute-start | bytes 393224 | tf_op jit(solution)/shard_map/ppermute | solution.py:227
  87.0 18.0 %all-to-all-start.3 = ((bf16[4,128,256]{2,1,0:T(8,128)(2,1)}), bf16[4,128,256]{2,1,0:T(8,128)(2,1)S(1)}, u32[]{:S(2)}, u32[]{:S(2)}) async-start(bf16[4,128,256]{2,1,0:T(8,128)(2,1)} %shard_map.96), calls=%async_computation.3 | async-start | bytes 524288 | tf_op jit(solution)/shard_map/all_to_all | solution.py:222
  93.6 11.4 %copy-start.2 = (bf16[128,256]{1,0:T(8,128)(2,1)S(1)}, bf16[128,256]{1,0:T(8,128)(2,1)}, u32[]{:S(2)}) copy-start(bf16[128,256]{1,0:T(8,128)(2,1)} %feats.1) | copy-start | bytes 196612
  93.6 11.4 %copy-start.3 = (bf16[256,256]{1,0:T(8,128)(2,1)S(1)}, bf16[256,256]{1,0:T(8,128)(2,1)}, u32[]{:S(2)}) copy-start(bf16[256,256]{1,0:T(8,128)(2,1)} %w_self.1) | copy-start | bytes 393220
  93.6 11.4 %copy-start.4 = (bf16[256,256]{1,0:T(8,128)(2,1)S(1)}, bf16[256,256]{1,0:T(8,128)(2,1)}, u32[]{:S(2)}) copy-start(bf16[256,256]{1,0:T(8,128)(2,1)} %w_in.1) | copy-start | bytes 393220
  93.6 11.4 %copy-start.5 = (bf16[256,256]{1,0:T(8,128)(2,1)S(1)}, bf16[256,256]{1,0:T(8,128)(2,1)}, u32[]{:S(2)}) copy-start(bf16[256,256]{1,0:T(8,128)(2,1)} %w_out.1) | copy-start | bytes 393220
  93.6 11.4 %copy-start.8 = (f32[256]{0:T(256)S(1)}, f32[256]{0:T(256)}, u32[]{:S(2)}) copy-start(f32[256]{0:T(256)} %param.17) | copy-start | bytes 3076
  93.7 7.4 %collective-permute-start.6 = (bf16[1,128,256]{2,1,0:T(8,128)(2,1)S(1)}, bf16[1,128,256]{2,1,0:T(8,128)(2,1)S(1)}, u32[]{:S(2)}, u32[]{:S(2)}) collective-permute-start(bf16[1,128,256]{2,1,0:T(8,128)(2,1)S(1)} %get-tuple-element.24), channel_id=1, source_target_pairs={{0,1},{1,0},{2,3},{3,2},{4,5},{5,4},{6,7},{7,6},{8,9},{9,8},{10,11... | collective-permute-start | bytes 196616 | tf_op jit(solution)/shard_map/ppermute | solution.py:227

commit v6 on v5

--- a/solution.py
+++ b/solution.py
@@ -8,7 +8,7 @@
 from jax.sharding import Mesh, PartitionSpec as P
 
 ZH, X, CORE, YQ, YP, ZL = "zh", "x", "core", "yq", "yp", "zl"
-UNROLL = 48
+UNROLL = 96
 COST = 20000
 COST2 = 40000
 TIE_COST = 10**11
@@ -122,20 +122,28 @@
     out[...] = jnp.maximum(total + bias[...], 0.0).astype(out.dtype)
 
 
-def copies_kernel(value, *refs):
-    out = refs[-1]
-    size = value.shape[0]
-    for k in range(out.shape[0] // size):
-        out[k * size : (k + 1) * size] = value[...]
+def copies_kernel(value, _, out, held, loaded, done):
+    load = pltpu.make_async_copy(value, held, loaded)
+    load.start()
+    load.wait()
+    copies = [pltpu.make_async_copy(held, out.at[k], done.at[k]) for k in range(out.shape[0])]
+    for copy in copies:
+        copy.start()
+    for copy in copies:
+        copy.wait()
 
 
 def copies_call(value, count, after):
     return pl.pallas_call(
         copies_kernel,
-        out_shape=jax.ShapeDtypeStruct((count * value.shape[0], *value.shape[1:]), value.dtype),
-        in_specs=[VMEM, ANY],
-        out_specs=VMEM,
-        compiler_params=pltpu.CompilerParams(vmem_limit_bytes=VMEM_LIMIT),
+        out_shape=jax.ShapeDtypeStruct((count, *value.shape), value.dtype),
+        in_specs=[ANY, ANY],
+        out_specs=ANY,
+        scratch_shapes=[
+            pltpu.VMEM(value.shape, value.dtype),
+            pltpu.SemaphoreType.DMA,
+            pltpu.SemaphoreType.DMA((count,)),
+        ],
         cost_estimate=pl.CostEstimate(
             flops=0, bytes_accessed=2 * (count + 1) * value.size, transcendentals=0
         ),
@@ -234,7 +242,7 @@
     scalars = jnp.stack([tile_count[0, 0], lax.axis_index(CORE), own_col]).astype(jnp.int32)
 
     near_row = lax.all_gather(feats, ZL)
-    near_col = exchange(copies_call(feats[None], 16, near_row), (ZH, X))
+    near_col = exchange(copies_call(feats, 16, near_row), (ZH, X))
     near_row = lax.all_gather(near_row, YQ, axis=0, tiled=True)
     far_row = tie_call(swap(near_row, YP, 1), (), TIE_COST)
     far_col = swap(near_col, CORE, 1)

time: 107 us -> 110 us (1.028)
  the two profiles are of different devices: /device:TPU:24 before, /device:TPU:8 now
where the time goes in v6:
time: 110 us; the launch traced here: 109 us
  starting transfers between devices  45.1 us (41%)
  blocking collectives  30.7 us (28%)
  waiting for transfers between devices  21 us (19%)
  Pallas kernels  11.3 us (10%)
    all_to_all x3, starting transfers between devices, exchange(): return lax.all_to_all(parts, axis, 0, 0, tiled=True)  23.3 us
    ppermute x7, starting transfers between devices, swap(): return lax.ppermute(value, axis, [(i, i ^ bit) for i in range(size)])  21.8 us
    all_gather x1, blocking collectives, per_device(): near_row = lax.all_gather(near_row, YQ, axis=0, tiled=True)  18.3 us
    all_to_all x3, waiting for transfers between devices, exchange(): return lax.all_to_all(parts, axis, 0, 0, tiled=True)  12.7 us
    ppermute x7, waiting for transfers between devices, swap(): return lax.ppermute(value, axis, [(i, i ^ bit) for i in range(size)])  8.22 us
    all_gather x1, blocking collectives, per_device(): near_row = lax.all_gather(feats, ZL)  7.03 us
    pallas_call x2, Pallas kernels, spmm_call(): pl.pallas_call(functools.partial(kernel, len(parts)), out_shape=[part] *...  6.16 us
    all_to_all x1, blocking collectives, exchange(): return lax.all_to_all(parts, axis, 0, 0, tiled=True)  5.41 us
  transfers between devices with their start and end apart: 10, of which 7 were waited for; matrix products, arithmetic and copies ran while one was open for 0% of the time, Pallas kernels for 5%

profile of v6, /device:TPU:8, one launch (start us, length us, event | category | flops | bytes accessed | tf_op | source)
XLA Modules:
  0.0 109.0 jit_solution(17644699510572347113)
XLA Ops:
  0.0 7.0 %all-gather = bf16[256,256]{1,0:T(8,128)(2,1)} all-gather(bf16[128,256]{1,0:T(8,128)(2,1)} %feats.1), channel_id=2, replica_groups=mesh['zh'=4,'x'=4,'core'=2,'yq'=4,'yp'=2,'zl'=2] {'zl'}, dimensions={0}, use_global_device_ids=true | all-gather | bytes 196608 | tf_op jit(solution)/shard_map/all_gather | solution.py:244
  7.0 2.0 %shard_map.92 = bf16[16,128,256]{2,1,0:T(8,128)(2,1)} custom-call(bf16[128,256]{1,0:T(8,128)(2,1)} %feats.1, bf16[2,128,256]{2,1,0:T(8,128)(2,1)} %bitcast.16), custom_call_target="tpu_custom_call" | custom-call | bytes 1114112 | tf_op jit(solution)/shard_map/pallas_call | solution.py:137
  9.1 12.0 %all-to-all-start = ((bf16[16,128,256]{2,1,0:T(8,128)(2,1)}), bf16[16,128,256]{2,1,0:T(8,128)(2,1)S(1)}, u32[]{:S(2)}, u32[]{:S(2)}) async-start(bf16[16,128,256]{2,1,0:T(8,128)(2,1)} %shard_map.92), calls=%async_computation | async-start | bytes 2097152 | tf_op jit(solution)/shard_map/all_to_all | solution.py:230
  21.1 18.3 %all_gather.11.refs_0_ = bf16[8,128,256]{2,1,0:T(8,128)(2,1)S(1)} all-gather(bf16[2,128,256]{2,1,0:T(8,128)(2,1)S(1)} %bitcast.17), channel_id=1, replica_groups=mesh['zh'=4,'x'=4,'core'=2,'yq'=4,'yp'=2,'zl'=2] {'yq'}, dimensions={0}, use_global_device_ids=true | all-gather | bytes 655360 | tf_op jit(solution)/shard_map/all_gather | solution.py:246
  39.4 3.3 %collective-permute-start = (bf16[8,128,256]{2,1,0:T(8,128)(2,1)S(1)}, bf16[8,128,256]{2,1,0:T(8,128)(2,1)S(1)}, u32[]{:S(2)}, u32[]{:S(2)}) collective-permute-start(bf16[8,128,256]{2,1,0:T(8,128)(2,1)S(1)} %all_gather.11.refs_0_), channel_id=1, source_target_pairs={{0,2},{2,0},{1,3},{3,1},{4,6},{6,4},{5,7},{7,5},{8,10},{10,8},{9,1... | collective-permute-start | bytes 1572872 | tf_op jit(solution)/shard_map/ppermute | solution.py:235
  43.4 6.3 %all-to-all-done.refs_0_ = bf16[16,128,256]{2,1,0:T(8,128)(2,1)S(1)} async-done(((bf16[16,128,256]{2,1,0:T(8,128)(2,1)}), bf16[16,128,256]{2,1,0:T(8,128)(2,1)S(1)}, u32[]{:S(2)}, u32[]{:S(2)}) %all-to-all-start) | async-done | bytes 1048608 | tf_op jit(solution)/shard_map/all_to_all | solution.py:230
  49.7 1.9 %collective-permute-start.1 = (bf16[16,128,256]{2,1,0:T(8,128)(2,1)S(1)}, bf16[16,128,256]{2,1,0:T(8,128)(2,1)S(1)}, u32[]{:S(2)}, u32[]{:S(2)}) collective-permute-start(bf16[16,128,256]{2,1,0:T(8,128)(2,1)S(1)} %all-to-all-done.refs_0_), channel_id=1, source_target_pairs={{0,16},{16,0},{1,17},{17,1},{2,18},{18,2},{3,19},{19,3},{4,20},{20... | collective-permute-start | bytes 3145736 | tf_op jit(solution)/shard_map/ppermute | solution.py:235
  52.0 2.2 %collective-permute-done.1.refs_1_ = bf16[16,128,256]{2,1,0:T(8,128)(2,1)S(1)} collective-permute-done((bf16[16,128,256]{2,1,0:T(8,128)(2,1)S(1)}, bf16[16,128,256]{2,1,0:T(8,128)(2,1)S(1)}, u32[]{:S(2)}, u32[]{:S(2)}) %collective-permute-start.1) | collective-permute-done | bytes 1048608 | tf_op jit(solution)/shard_map/ppermute | solution.py:235
  54.2 2.8 %shard_map.93 = (bf16[8,128,256]{2,1,0:T(8,128)(2,1)S(1)}, bf16[8,128,256]{2,1,0:T(8,128)(2,1)S(1)}, f32[8,128]{1,0:T(8,128)S(1)}) custom-call(s32[3]{0:T(128)S(1)} %pad_add_fusion.scalars, s32[96]{0:T(128)S(1)} %bitcast.11, s32[96]{0:T(128)S(1)} %bitcast.13, bf16[96,128,128]{2,1,0:T(8,128)(2,1)S(1)} %bitcast.9, ...), custom_call_target="tpu_custom_call" | custom-call | flops 805306368 | bytes 8388608 | tf_op jit(solution)/shard_map/pallas_call | solution.py:194
  57.0 2.4 %collective-permute-start.2 = (bf16[8,128,256]{2,1,0:T(8,128)(2,1)S(1)}, bf16[8,128,256]{2,1,0:T(8,128)(2,1)S(1)}, u32[]{:S(2)}, u32[]{:S(2)}) collective-permute-start(bf16[8,128,256]{2,1,0:T(8,128)(2,1)S(1)} %get-tuple-element.18), channel_id=1, source_target_pairs={{0,2},{2,0},{1,3},{3,1},{4,6},{6,4},{5,7},{7,5},{8,10},{10,8},{9,1... | collective-permute-start | bytes 1572872 | tf_op jit(solution)/shard_map/ppermute | solution.py:235
  59.3 3.4 %shard_map.94 = (bf16[32,128,256]{2,1,0:T(8,128)(2,1)S(1)}, f32[8,128]{1,0:T(8,128)}) custom-call(s32[3]{0:T(128)S(1)} %pad_add_fusion.scalars, s32[96]{0:T(128)S(1)} %bitcast.12, s32[96]{0:T(128)S(1)} %bitcast.14, bf16[96,128,128]{2,1,0:T(8,128)(2,1)S(1)} %bitcast.10, bf16[8,128,256]{2,1,0:T(8,128)(2,1)S(1)} %all_gather.11.refs_0_, ...), custom_call_target="tpu_custom_call" | custom-call | flops 805306368 | bytes 8388608 | tf_op jit(solution)/shard_map/pallas_call | solution.py:194
  62.7 5.4 %all_to_all.20.parts = bf16[32,128,256]{2,1,0:T(8,128)(2,1)S(1)} all-to-all(bf16[32,128,256]{2,1,0:T(8,128)(2,1)S(1)} %get-tuple-element.16), channel_id=1, replica_groups=mesh['zh'=4,'x'=4,'core'=2,'yq'=4,'yp'=2,'zl'=2] {'core'}, dimensions={0} | all-to-all | bytes 4194304 | tf_op jit(solution)/shard_map/all_to_all | solution.py:230
  68.1 1.2 %shard_map.95 = bf16[16,128,256]{2,1,0:T(8,128)(2,1)} custom-call(bf16[32,128,256]{2,1,0:T(8,128)(2,1)S(1)} %all_to_all.20.parts), custom_call_target="tpu_custom_call" | custom-call | flops 1048576 | bytes 3145728 | tf_op jit(solution)/shard_map/pallas_call | solution.py:179
  69.4 4.3 %all-to-all-start.2 = ((bf16[16,128,256]{2,1,0:T(8,128)(2,1)}), bf16[16,128,256]{2,1,0:T(8,128)(2,1)S(1)}, u32[]{:S(2)}, u32[]{:S(2)}) async-start(bf16[16,128,256]{2,1,0:T(8,128)(2,1)} %shard_map.95), calls=%async_computation.2 | async-start | bytes 2097152 | tf_op jit(solution)/shard_map/all_to_all | solution.py:230
  73.8 3.7 %collective-permute-start.3 = (bf16[2,128,256]{2,1,0:T(8,128)(2,1)S(1)}, bf16[2,128,256]{2,1,0:T(8,128)(2,1)S(1)}, u32[]{:S(2)}, u32[]{:S(2)}) collective-permute-start(bf16[2,128,256]{2,1,0:T(8,128)(2,1)S(1)} %get-tuple-element.20), channel_id=1, source_target_pairs={{0,4},{4,0},{8,12},{12,8},{1,5},{5,1},{9,13},{13,9},{2,6},{6,2},{1... | collective-permute-start | bytes 393224 | tf_op jit(solution)/shard_map/ppermute | solution.py:235
  77.6 5.9 %collective-permute-start.4 = (bf16[2,128,256]{2,1,0:T(8,128)(2,1)S(1)}, bf16[2,128,256]{2,1,0:T(8,128)(2,1)S(1)}, u32[]{:S(2)}, u32[]{:S(2)}) collective-permute-start(bf16[2,128,256]{2,1,0:T(8,128)(2,1)S(1)} %get-tuple-element.21), channel_id=1, source_target_pairs={{0,8},{4,12},{8,0},{12,4},{1,9},{5,13},{9,1},{13,5},{2,10},{6,14},... | collective-permute-start | bytes 393224 | tf_op jit(solution)/shard_map/ppermute | solution.py:235
  83.5 2.6 %collective-permute-start.5 = (bf16[2,128,256]{2,1,0:T(8,128)(2,1)S(1)}, bf16[2,128,256]{2,1,0:T(8,128)(2,1)S(1)}, u32[]{:S(2)}, u32[]{:S(2)}) collective-permute-start(bf16[2,128,256]{2,1,0:T(8,128)(2,1)S(1)} %get-tuple-element.22), channel_id=1, source_target_pairs={{0,12},{4,8},{8,4},{12,0},{1,13},{5,9},{9,5},{13,1},{2,14},{6,10},... | collective-permute-start | bytes 393224 | tf_op jit(solution)/shard_map/ppermute | solution.py:235
  86.1 3.0 %all-to-all-done.2.parts = bf16[16,128,256]{2,1,0:T(8,128)(2,1)S(1)} async-done(((bf16[16,128,256]{2,1,0:T(8,128)(2,1)}), bf16[16,128,256]{2,1,0:T(8,128)(2,1)S(1)}, u32[]{:S(2)}, u32[]{:S(2)}) %all-to-all-start.2) | async-done | bytes 1048608 | tf_op jit(solution)/shard_map/all_to_all | solution.py:230
  89.1 0.8 shard_map.96
  89.9 6.9 %all-to-all-start.3 = ((bf16[4,128,256]{2,1,0:T(8,128)(2,1)}), bf16[4,128,256]{2,1,0:T(8,128)(2,1)S(1)}, u32[]{:S(2)}, u32[]{:S(2)}) async-start(bf16[4,128,256]{2,1,0:T(8,128)(2,1)} %shard_map.96), calls=%async_computation.3 | async-start | bytes 524288 | tf_op jit(solution)/shard_map/all_to_all | solution.py:230
  97.7 2.1 %collective-permute-start.6 = (bf16[1,128,256]{2,1,0:T(8,128)(2,1)S(1)}, bf16[1,128,256]{2,1,0:T(8,128)(2,1)S(1)}, u32[]{:S(2)}, u32[]{:S(2)}) collective-permute-start(bf16[1,128,256]{2,1,0:T(8,128)(2,1)S(1)} %get-tuple-element.24), channel_id=1, source_target_pairs={{0,1},{1,0},{2,3},{3,2},{4,5},{5,4},{6,7},{7,6},{8,9},{9,8},{10,11... | collective-permute-start | bytes 196616 | tf_op jit(solution)/shard_map/ppermute | solution.py:235
  99.8 4.9 %collective-permute-done.6.refs_1_ = bf16[1,128,256]{2,1,0:T(8,128)(2,1)S(1)} collective-permute-done((bf16[1,128,256]{2,1,0:T(8,128)(2,1)S(1)}, bf16[1,128,256]{2,1,0:T(8,128)(2,1)S(1)}, u32[]{:S(2)}, u32[]{:S(2)}) %collective-permute-start.6) | collective-permute-done | bytes 65568 | tf_op jit(solution)/shard_map/ppermute | solution.py:235
  104.7 3.4 %all-to-all-done.3.terms_out = bf16[4,128,256]{2,1,0:T(8,128)(2,1)S(1)} async-done(((bf16[4,128,256]{2,1,0:T(8,128)(2,1)}), bf16[4,128,256]{2,1,0:T(8,128)(2,1)S(1)}, u32[]{:S(2)}, u32[]{:S(2)}) %all-to-all-start.3) | async-done | bytes 262176 | tf_op jit(solution)/shard_map/all_to_all | solution.py:230
  108.1 0.9 shard_map.99
  (27 shorter events, 1.4 us)
Async XLA Ops:
  7.0 14.0 %copy-start.8 = (bf16[256,256]{1,0:T(8,128)(2,1)S(1)}, bf16[256,256]{1,0:T(8,128)(2,1)}, u32[]{:S(2)}) copy-start(bf16[256,256]{1,0:T(8,128)(2,1)} %all-gather) | copy-start | bytes 393220
  9.1 40.6 %all-to-all-start = ((bf16[16,128,256]{2,1,0:T(8,128)(2,1)}), bf16[16,128,256]{2,1,0:T(8,128)(2,1)S(1)}, u32[]{:S(2)}, u32[]{:S(2)}) async-start(bf16[16,128,256]{2,1,0:T(8,128)(2,1)} %shard_map.92), calls=%async_computation | async-start | bytes 2097152 | tf_op jit(solution)/shard_map/all_to_all | solution.py:230
  39.4 12.6 %collective-permute-start = (bf16[8,128,256]{2,1,0:T(8,128)(2,1)S(1)}, bf16[8,128,256]{2,1,0:T(8,128)(2,1)S(1)}, u32[]{:S(2)}, u32[]{:S(2)}) collective-permute-start(bf16[8,128,256]{2,1,0:T(8,128)(2,1)S(1)} %all_gather.11.refs_0_), channel_id=1, source_target_pairs={{0,2},{2,0},{1,3},{3,1},{4,6},{6,4},{5,7},{7,5},{8,10},{10,8},{9,1... | collective-permute-start | bytes 1572872 | tf_op jit(solution)/shard_map/ppermute | solution.py:235
  43.4 10.8 %copy-start.5 = (s32[1,1,96]{2,1,0:T(1,128)S(1)}, s32[1,1,96]{2,1,0:T(1,128)}, u32[]{:S(2)}) copy-start(s32[1,1,96]{2,1,0:T(1,128)} %param.11) | copy-start | bytes 1156
  43.4 10.8 %copy-start.6 = (s32[1,1,96]{2,1,0:T(1,128)S(1)}, s32[1,1,96]{2,1,0:T(1,128)}, u32[]{:S(2)}) copy-start(s32[1,1,96]{2,1,0:T(1,128)} %param.12) | copy-start | bytes 1156
  49.7 4.5 %collective-permute-start.1 = (bf16[16,128,256]{2,1,0:T(8,128)(2,1)S(1)}, bf16[16,128,256]{2,1,0:T(8,128)(2,1)S(1)}, u32[]{:S(2)}, u32[]{:S(2)}) collective-permute-start(bf16[16,128,256]{2,1,0:T(8,128)(2,1)S(1)} %all-to-all-done.refs_0_), channel_id=1, source_target_pairs={{0,16},{16,0},{1,17},{17,1},{2,18},{18,2},{3,19},{19,3},{4,20},{20... | collective-permute-start | bytes 3145736 | tf_op jit(solution)/shard_map/ppermute | solution.py:235
  51.9 2.3 %copy-start = (bf16[1,1,96,128,128]{4,3,2,1,0:T(8,128)(2,1)S(1)}, bf16[1,1,96,128,128]{4,3,2,1,0:T(8,128)(2,1)}, u32[]{:S(2)}) copy-start(bf16[1,1,96,128,128]{4,3,2,1,0:T(8,128)(2,1)} %param.10) | copy-start | bytes 9437188
  57.0 16.8 %collective-permute-start.2 = (bf16[8,128,256]{2,1,0:T(8,128)(2,1)S(1)}, bf16[8,128,256]{2,1,0:T(8,128)(2,1)S(1)}, u32[]{:S(2)}, u32[]{:S(2)}) collective-permute-start(bf16[8,128,256]{2,1,0:T(8,128)(2,1)S(1)} %get-tuple-element.18), channel_id=1, source_target_pairs={{0,2},{2,0},{1,3},{3,1},{4,6},{6,4},{5,7},{7,5},{8,10},{10,8},{9,1... | collective-permute-start | bytes 1572872 | tf_op jit(solution)/shard_map/ppermute | solution.py:235
  69.4 19.7 %all-to-all-start.2 = ((bf16[16,128,256]{2,1,0:T(8,128)(2,1)}), bf16[16,128,256]{2,1,0:T(8,128)(2,1)S(1)}, u32[]{:S(2)}, u32[]{:S(2)}) async-start(bf16[16,128,256]{2,1,0:T(8,128)(2,1)} %shard_map.95), calls=%async_computation.2 | async-start | bytes 2097152 | tf_op jit(solution)/shard_map/all_to_all | solution.py:230
  73.8 23.0 %collective-permute-start.3 = (bf16[2,128,256]{2,1,0:T(8,128)(2,1)S(1)}, bf16[2,128,256]{2,1,0:T(8,128)(2,1)S(1)}, u32[]{:S(2)}, u32[]{:S(2)}) collective-permute-start(bf16[2,128,256]{2,1,0:T(8,128)(2,1)S(1)} %get-tuple-element.20), channel_id=1, source_target_pairs={{0,4},{4,0},{8,12},{12,8},{1,5},{5,1},{9,13},{13,9},{2,6},{6,2},{1... | collective-permute-start | bytes 393224 | tf_op jit(solution)/shard_map/ppermute | solution.py:235
  77.6 19.3 %collective-permute-start.4 = (bf16[2,128,256]{2,1,0:T(8,128)(2,1)S(1)}, bf16[2,128,256]{2,1,0:T(8,128)(2,1)S(1)}, u32[]{:S(2)}, u32[]{:S(2)}) collective-permute-start(bf16[2,128,256]{2,1,0:T(8,128)(2,1)S(1)} %get-tuple-element.21), channel_id=1, source_target_pairs={{0,8},{4,12},{8,0},{12,4},{1,9},{5,13},{9,1},{13,5},{2,10},{6,14},... | collective-permute-start | bytes 393224 | tf_op jit(solution)/shard_map/ppermute | solution.py:235
  83.5 14.1 %collective-permute-start.5 = (bf16[2,128,256]{2,1,0:T(8,128)(2,1)S(1)}, bf16[2,128,256]{2,1,0:T(8,128)(2,1)S(1)}, u32[]{:S(2)}, u32[]{:S(2)}) collective-permute-start(bf16[2,128,256]{2,1,0:T(8,128)(2,1)S(1)} %get-tuple-element.22), channel_id=1, source_target_pairs={{0,12},{4,8},{8,4},{12,0},{1,13},{5,9},{9,5},{13,1},{2,14},{6,10},... | collective-permute-start | bytes 393224 | tf_op jit(solution)/shard_map/ppermute | solution.py:235
  89.9 18.2 %all-to-all-start.3 = ((bf16[4,128,256]{2,1,0:T(8,128)(2,1)}), bf16[4,128,256]{2,1,0:T(8,128)(2,1)S(1)}, u32[]{:S(2)}, u32[]{:S(2)}) async-start(bf16[4,128,256]{2,1,0:T(8,128)(2,1)} %shard_map.96), calls=%async_computation.3 | async-start | bytes 524288 | tf_op jit(solution)/shard_map/all_to_all | solution.py:230
  97.6 10.5 %copy-start.1 = (bf16[128,256]{1,0:T(8,128)(2,1)S(1)}, bf16[128,256]{1,0:T(8,128)(2,1)}, u32[]{:S(2)}) copy-start(bf16[128,256]{1,0:T(8,128)(2,1)} %feats.1) | copy-start | bytes 196612
  97.6 10.5 %copy-start.2 = (bf16[256,256]{1,0:T(8,128)(2,1)S(1)}, bf16[256,256]{1,0:T(8,128)(2,1)}, u32[]{:S(2)}) copy-start(bf16[256,256]{1,0:T(8,128)(2,1)} %w_self.1) | copy-start | bytes 393220
  97.6 10.5 %copy-start.3 = (bf16[256,256]{1,0:T(8,128)(2,1)S(1)}, bf16[256,256]{1,0:T(8,128)(2,1)}, u32[]{:S(2)}) copy-start(bf16[256,256]{1,0:T(8,128)(2,1)} %w_in.1) | copy-start | bytes 393220
  97.6 10.5 %copy-start.4 = (bf16[256,256]{1,0:T(8,128)(2,1)S(1)}, bf16[256,256]{1,0:T(8,128)(2,1)}, u32[]{:S(2)}) copy-start(bf16[256,256]{1,0:T(8,128)(2,1)} %w_out.1) | copy-start | bytes 393220
  97.6 10.5 %copy-start.7 = (f32[256]{0:T(256)S(1)}, f32[256]{0:T(256)}, u32[]{:S(2)}) copy-start(f32[256]{0:T(256)} %param.17) | copy-start | bytes 3076
  97.7 7.0 %collective-permute-start.6 = (bf16[1,128,256]{2,1,0:T(8,128)(2,1)S(1)}, bf16[1,128,256]{2,1,0:T(8,128)(2,1)S(1)}, u32[]{:S(2)}, u32[]{:S(2)}) collective-permute-start(bf16[1,128,256]{2,1,0:T(8,128)(2,1)S(1)} %get-tuple-element.24), channel_id=1, source_target_pairs={{0,1},{1,0},{2,3},{3,2},{4,5},{5,4},{6,7},{7,6},{8,9},{9,8},{10,11... | collective-permute-start | bytes 196616 | tf_op jit(solution)/shard_map/ppermute | solution.py:235
